TPU v7x, 256 devices: a whole 4x4x8 slice. The times are simulated.
256 devices in a mesh: section: 4 (over z_lo), rep: 8 (over z_hi, x), tp: 8 (over y, core).
Axes of the slice: x: 4, y: 4, z: 8 (z_hi: 2, z_lo: 4; z = z_hi * 4 + z_lo), core: 2. Of those that a mesh axis runs over, the one named last changes fastest.
Arguments:
- prefill_query: bfloat16 [256, 256, 4096], P(('section', 'rep'), None, 'tp'), may hold values from -1.0546875 to 1.0546875
- prefill_key: bfloat16 [256, 256, 4096], P(('section', 'rep'), None, 'tp'), may hold values from -1.0546875 to 1.0546875
- prefill_value: bfloat16 [256, 256, 4096], P(('section', 'rep'), None, 'tp'), may hold values from -6 to 6
- prefill_gate: float32 [256, 256, 32], P(('section', 'rep'), None, 'tp'), may hold values from 0.45 to 1
- lengths: int32 [256], replicated, may hold values from 1 to 256, 40960 in all
- decode_group: int32 [256], replicated, may hold values from 0 to 31, as said below
- cache_keys: bfloat16 [256, 256, 1024], P(('section', 'rep'), None, 'tp'), may hold values from -6 to 6
- cache_values: bfloat16 [256, 256, 1024], P(('section', 'rep'), None, 'tp'), may hold values from -6 to 6
- out_weight: bfloat16 [4096, 6144], P('tp'), may hold values from -0.09375 to 0.09375
- norm_gain: float32 [6144], replicated, may hold values from 0.25 to 1.75
- step_input: bfloat16 [4, 256, 6144], P(None, ('section', 'rep')), may hold values from -3 to 3
- step_query: bfloat16 [4, 256, 4096], P(None, ('section', 'rep'), 'tp'), may hold values from -1.0546875 to 1.0546875
- step_key: bfloat16 [4, 256, 4096], P(None, ('section', 'rep'), 'tp'), may hold values from -1.0546875 to 1.0546875
- step_value: bfloat16 [4, 256, 4096], P(None, ('section', 'rep'), 'tp'), may hold values from -6 to 6
- step_gate: float32 [4, 256, 32], P(None, ('section', 'rep'), 'tp'), may hold values from 0.5 to 1
- soft_query: bfloat16 [4, 256, 8192], P(None, ('section', 'rep'), 'tp'), may hold values from -50 to 50
- soft_new_key: bfloat16 [4, 256, 1024], P(None, ('section', 'rep'), 'tp'), may hold values from -4 to 4
- soft_new_value: bfloat16 [4, 256, 1024], P(None, ('section', 'rep'), 'tp'), may hold values from -6 to 6
Outputs:
- prefill_out: bfloat16 [256, 256, 4096], P(('section', 'rep'), None, 'tp')
- decode_out: bfloat16 [4, 256, 6144], P(None, ('section', 'rep'))
- soft_out: bfloat16 [4, 256, 8192], P(None, ('section', 'rep'), 'tp')
Inputs may be any that keep to these rules, and one draw needn't show every extreme that they name: `decode_group`: request group g holds requests g * 8 to g * 8 + 7; a group g has section index g // 8 and rep index g % 8. Every group receives exactly 8 requests. The requests of one group name each rep index exactly 8 / 8 times and each section index exactly 8 / 4 times. The requests that leave the groups of one section index for groups of one rep index name each section index exactly 8 / 4 times; the requests that leave the groups of one rep index for groups of one section index name each rep index exactly 8 / 8 times.
All inputs are finite; a program needn't handle non-finite values.
Results may differ from a plain program's by a relative error of at most 0.0049.
Values may be sent and summed in bfloat16 or wider, within the bound.
A program may use at most 64 MiB of HBM per device.

v0:
```python
import math

import jax
import jax.numpy as jnp
from jax import lax
from jax.sharding import PartitionSpec as P

HIGHEST = lax.Precision.HIGHEST


def normalize(summed, norm_gain):
    spread = jnp.sqrt(jnp.mean(summed * summed, axis=-1, keepdims=True) + 1e-06)
    return (summed / spread * norm_gain).astype(jnp.bfloat16)


def ranked(selected, sort_keys, count):
    numbers = jnp.arange(selected.shape[0], dtype=jnp.int32)
    before = selected[None, :] & (sort_keys[None, :] < sort_keys[:, None])
    rank_of = jnp.sum(before.astype(jnp.int32), axis=1)
    places = jnp.arange(count, dtype=jnp.int32)
    hit = selected[None, :] & (rank_of[None, :] == places[:, None])
    return jnp.sum(jnp.where(hit, numbers[None, :], 0), axis=1)


def positions(wanted, held_ids):
    places = jnp.arange(held_ids.shape[0], dtype=jnp.int32)
    match = wanted[:, None] == held_ids[None, :]
    return jnp.sum(jnp.where(match, places[None, :], 0), axis=1)


def reorder(parts, index):
    return tuple((jnp.take(piece, index, axis=0) for piece in parts))


def blocked(piece, count):
    return piece.reshape((count, -1) + piece.shape[1:])


def rep_leg(parts):
    count = lax.axis_size("rep")
    states, keys_part, values_part = parts
    moved = lax.all_to_all(
        blocked(states, count), "rep", split_axis=0, concat_axis=0, tiled=True
    ).reshape(states.shape)
    cache = (
        lax.all_to_all(blocked(keys_part, count), "rep", split_axis=0, concat_axis=0, tiled=True),
        lax.all_to_all(blocked(values_part, count), "rep", split_axis=0, concat_axis=0, tiled=True),
    )
    return (moved, cache[0].reshape(keys_part.shape), cache[1].reshape(values_part.shape))


def section_leg(parts):
    count = lax.axis_size("section")
    states, keys_part, values_part = parts
    moved = lax.all_to_all(
        blocked(states, count), "section", split_axis=0, concat_axis=0, tiled=True
    ).reshape(states.shape)
    cache = (
        lax.all_to_all(
            blocked(keys_part, count), "section", split_axis=0, concat_axis=0, tiled=True
        ),
        lax.all_to_all(
            blocked(values_part, count), "section", split_axis=0, concat_axis=0, tiled=True
        ),
    )
    return (moved, cache[0].reshape(keys_part.shape), cache[1].reshape(values_part.shape))


def on_device(
    prefill_query,
    prefill_key,
    prefill_value,
    prefill_gate,
    lengths,
    decode_group,
    cache_keys,
    cache_values,
    out_weight,
    norm_gain,
    step_input,
    step_query,
    step_key,
    step_value,
    step_gate,
    soft_query,
    soft_new_key,
    soft_new_value,
):
    held = prefill_query.shape[0]
    length = prefill_query.shape[1]
    heads = prefill_gate.shape[2]
    head_size = prefill_query.shape[2] // heads
    kv_heads = cache_keys.shape[2] // head_size
    query_heads = soft_query.shape[2] // head_size
    steps_all = step_query.shape[0]
    total = decode_group.shape[0]
    replicas = lax.axis_size("rep")
    my_section = lax.axis_index("section")
    my_rep = lax.axis_index("rep")
    group_no = my_section * replicas + my_rep
    numbers = jnp.arange(total, dtype=jnp.int32)
    own_lengths = lax.dynamic_slice_in_dim(lengths, group_no * held, held)
    places = jnp.arange(length, dtype=jnp.int32)
    inside = places[None, :] < own_lengths[:, None]
    cumlog = jnp.cumsum(jnp.where(inside[:, :, None], jnp.log(prefill_gate), 0.0), axis=1)
    decays = jnp.where(inside[:, :, None], jnp.exp(cumlog[:, -1:, :] - cumlog), 0.0)
    keys_four = prefill_key.reshape(held, length, heads, head_size)
    values_four = prefill_value.reshape(held, length, heads, head_size)
    weighted = decays[..., None] * keys_four.astype(jnp.float32)
    memories = jnp.einsum(
        "rshd,rshe->rhde", weighted, values_four.astype(jnp.float32), precision=HIGHEST
    )
    source_group = numbers // held
    source_section = source_group // replicas
    source_rep = source_group % replicas
    target_section = decode_group // replicas
    target_rep = decode_group % replicas
    mine_out = source_group == group_no
    mine_in = decode_group == group_no
    held_now = ranked(mine_out, numbers, held)
    parts = (memories, cache_keys, cache_values)
    send_first = ranked(mine_out, target_rep * total + numbers, held)
    parts = rep_leg(reorder(parts, positions(send_first, held_now)))
    middle = (source_section == my_section) & (target_rep == my_rep)
    held_now = ranked(middle, source_rep * total + numbers, held)
    send_second = ranked(middle, target_section * total + numbers, held)
    parts = section_leg(reorder(parts, positions(send_second, held_now)))
    held_now = ranked(mine_in, source_section * total + numbers, held)
    request_of = ranked(mine_in, numbers, held)
    carried, slot_keys, slot_values = reorder(parts, positions(request_of, held_now))
    queries_four = prefill_query.reshape(held, length, heads, head_size)
    scores = jnp.einsum(
        "rthd,rshd->rhts", queries_four, keys_four, preferred_element_type=jnp.float32
    )
    heads_first = jnp.transpose(cumlog, (0, 2, 1))
    gaps = heads_first[:, :, :, None] - heads_first[:, :, None, :]
    causal = places[:, None] >= places[None, :]
    keeping = causal[None, None] & inside[:, None, None, :] & inside[:, None, :, None]
    weights = jnp.where(keeping, jnp.exp(jnp.where(keeping, gaps, 0.0)) * scores, 0.0).astype(
        jnp.bfloat16
    )
    prefill_out = jnp.einsum(
        "rhts,rshd->rthd", weights, values_four, preferred_element_type=jnp.float32
    )
    prefill_out = prefill_out.astype(jnp.bfloat16).reshape(held, length, heads * head_size)
    slot_lengths = jnp.take(lengths, request_of)
    slot_keys = slot_keys.reshape(held, length, kv_heads, head_size)
    slot_values = slot_values.reshape(held, length, kv_heads, head_size)
    fresh_keys = soft_new_key.reshape(steps_all, held, kv_heads, head_size)
    fresh_values = soft_new_value.reshape(steps_all, held, kv_heads, head_size)
    cache_ok = places[None, :] < slot_lengths[:, None]
    score_scale = 1.0 / math.sqrt(head_size)
    group_size = query_heads // kv_heads
    linear_rows = []
    soft_rows = []
    for step_no in range(steps_all):
        key_now = step_key[step_no].reshape(held, heads, head_size).astype(jnp.float32)
        value_now = step_value[step_no].reshape(held, heads, head_size).astype(jnp.float32)
        query_now = step_query[step_no].reshape(held, heads, head_size).astype(jnp.float32)
        carried = (
            step_gate[step_no][:, :, None, None] * carried
            + key_now[:, :, :, None] * value_now[:, :, None, :]
        )
        linear = jnp.einsum("rhd,rhde->rhe", query_now, carried, precision=HIGHEST)
        linear_rows.append(linear.reshape(held, heads * head_size).astype(jnp.bfloat16))
        asked = soft_query[step_no].reshape(held, kv_heads, group_size, head_size)
        cache_scores = (
            jnp.einsum("rkgd,rskd->rkgs", asked, slot_keys, preferred_element_type=jnp.float32)
            * score_scale
        )
        fresh_scores = (
            jnp.einsum("rkgd,nrkd->rkgn", asked, fresh_keys, preferred_element_type=jnp.float32)
            * score_scale
        )
        cache_scores = jnp.where(cache_ok[:, None, None, :], cache_scores, -jnp.inf)
        fresh_ok = jnp.arange(steps_all, dtype=jnp.int32) <= step_no
        fresh_scores = jnp.where(fresh_ok, fresh_scores, -jnp.inf)
        peaks = jnp.maximum(jnp.max(cache_scores, axis=-1), jnp.max(fresh_scores, axis=-1))
        cache_exp = jnp.exp(cache_scores - peaks[..., None])
        fresh_exp = jnp.exp(fresh_scores - peaks[..., None])
        denominator = jnp.sum(cache_exp, axis=-1) + jnp.sum(fresh_exp, axis=-1)
        cache_prob = (cache_exp / denominator[..., None]).astype(jnp.bfloat16)
        fresh_prob = (fresh_exp / denominator[..., None]).astype(jnp.bfloat16)
        mixed = jnp.einsum(
            "rkgs,rskd->rkgd", cache_prob, slot_values, preferred_element_type=jnp.float32
        )
        mixed = mixed + jnp.einsum(
            "rkgn,nrkd->rkgd", fresh_prob, fresh_values, preferred_element_type=jnp.float32
        )
        soft_rows.append(mixed.reshape(held, query_heads * head_size).astype(jnp.bfloat16))
    linear_all = jnp.stack(linear_rows).reshape(steps_all * held, heads * head_size)
    soft_out = jnp.stack(soft_rows)
    residual = step_input.reshape(steps_all * held, -1)
    projected = jnp.dot(linear_all, out_weight, preferred_element_type=jnp.float32)
    summed = lax.psum(projected, "tp")
    decode_out = normalize(residual.astype(jnp.float32) + summed, norm_gain)
    decode_out = decode_out.reshape(steps_all, held, -1)
    return (prefill_out, decode_out, soft_out)


def solution(mesh):
    return jax.shard_map(
        on_device,
        mesh=mesh,
        in_specs=(
            P(("section", "rep"), None, "tp"),
            P(("section", "rep"), None, "tp"),
            P(("section", "rep"), None, "tp"),
            P(("section", "rep"), None, "tp"),
            P(),
            P(),
            P(("section", "rep"), None, "tp"),
            P(("section", "rep"), None, "tp"),
            P("tp", None),
            P(),
            P(None, ("section", "rep"), None),
            P(None, ("section", "rep"), "tp"),
            P(None, ("section", "rep"), "tp"),
            P(None, ("section", "rep"), "tp"),
            P(None, ("section", "rep"), "tp"),
            P(None, ("section", "rep"), "tp"),
            P(None, ("section", "rep"), "tp"),
            P(None, ("section", "rep"), "tp"),
        ),
        out_specs=(
            P(("section", "rep"), None, "tp"),
            P(None, ("section", "rep"), None),
            P(None, ("section", "rep"), "tp"),
        ),
        check_vma=False,
    )
```

profile of v0, /device:TPU:1, one launch (start us, length us, event | category | flops | bytes accessed | tf_op | source)
XLA Modules:
  0.0 297.1 jit_solution(4420661024336501520)
XLA Ops:
  8.6 1.7 gather_fusion.4
  10.4 1.7 gather_fusion.7
  13.2 11.5 %all-to-all-start.2 = ((bf16[8,1,256,128]{3,2,1,0:T(8,128)(2,1)}), bf16[8,1,256,128]{3,2,1,0:T(8,128)(2,1)S(1)}, u32[]{:S(2)}, u32[]{:S(2)}) async-start(bf16[8,1,256,128]{3,2,1,0:T(8,128)(2,1)} %get-tuple-element.60), calls=%async_computation.2 | async-start | bytes 1048576 | tf_op jit(solution)/shard_map/all_to_all | solution.py:46
  24.9 2.3 reduce-window.6
  27.7 3.9 %copy.184 = bf16[8,256,512]{1,2,0:T(8,128)(2,1)} copy(bf16[8,256,512]{2,1,0:T(8,128)(2,1)} %param.23) | data formatting | bytes 4194304 | tf_op jit(solution)/shard_map/reshape | solution.py:107
  32.6 3.6 %all-to-all-done.2 = bf16[8,1,256,128]{3,2,1,0:T(8,128)(2,1)S(1)} async-done(((bf16[8,1,256,128]{3,2,1,0:T(8,128)(2,1)}), bf16[8,1,256,128]{3,2,1,0:T(8,128)(2,1)S(1)}, u32[]{:S(2)}, u32[]{:S(2)}) %all-to-all-start.2) | async-done | bytes 524320 | tf_op jit(solution)/shard_map/all_to_all | solution.py:46
  36.3 5.4 %all-to-all-start.4 = ((bf16[8,1,256,128]{3,2,1,0:T(8,128)(2,1)}), bf16[8,1,256,128]{3,2,1,0:T(8,128)(2,1)}, u32[]{:S(2)}, u32[]{:S(2)}) async-start(bf16[8,1,256,128]{3,2,1,0:T(8,128)(2,1)} %get-tuple-element.59), calls=%async_computation.4 | async-start | bytes 1048576 | tf_op jit(solution)/shard_map/all_to_all | solution.py:47
  41.7 5.2 %fusion.1 = f32[8,4,128,128]{3,2,1,0:T(8,128)} fusion(bf16[8,256,4,128]{1,3,2,0:T(8,128)(2,1)} %bitcast.211, f32[8,256,4]{1,2,0:T(4,128)S(1)} %copy.152, bf16[8,256,512]{2,1,0:T(8,128)(2,1)S(1)} %copy-done), kind=kOutput, calls=%fused_computation.12 | convolution fusion | flops 1612709888 | bytes 6324224 | tf_op jit(solution)/shard_map/rshd,rshe->rhde/dot_general | solution.py:110
  47.6 5.3 %all-to-all-done.4 = bf16[8,1,256,128]{3,2,1,0:T(8,128)(2,1)} async-done(((bf16[8,1,256,128]{3,2,1,0:T(8,128)(2,1)}), bf16[8,1,256,128]{3,2,1,0:T(8,128)(2,1)}, u32[]{:S(2)}, u32[]{:S(2)}) %all-to-all-start.4) | async-done | bytes 524320 | tf_op jit(solution)/shard_map/all_to_all | solution.py:47
  53.0 1.7 gather_fusion.8
  55.8 11.1 %all-to-all-start.3 = ((bf16[4,2,256,128]{3,2,1,0:T(8,128)(2,1)}), bf16[4,2,256,128]{3,2,1,0:T(8,128)(2,1)S(1)}, u32[]{:S(2)}, u32[]{:S(2)}) async-start(bf16[4,2,256,128]{3,2,1,0:T(8,128)(2,1)} %bitcast.45), calls=%async_computation.3 | async-start | bytes 1048576 | tf_op jit(solution)/shard_map/all_to_all | solution.py:59
  66.9 3.6 %gather_fusion.1 = f32[8,4,128,128]{3,2,1,0:T(8,128)} fusion(f32[8,4,128,128]{3,2,1,0:T(8,128)} %fusion.1, s32[1024]{0:T(1024)S(1)} %pad_clamp_fusion.3), kind=kCustom, calls=%fused_computation.clone | custom fusion | bytes 4194336 | tf_op jit(solution)/shard_map/jit(_take)/gather | solution.py:32
  70.7 3.3 %select_bitcast_fusion = f32[8,1,4,128,128]{4,3,2,1,0:T(8,128)} fusion(f32[8,4,128,128]{3,2,1,0:T(8,128)} %gather_fusion.1, pred[8]{0:T(512)(128)(4,1)S(1)} %compare_and_fusion.2), kind=kLoop, calls=%fused_computation.26 | loop fusion | flops 524288 | bytes 4194312 | tf_op jit(solution)/shard_map/reshape | solution.py:36
  74.0 6.2 %all-to-all-done.3 = bf16[4,2,256,128]{3,2,1,0:T(8,128)(2,1)S(1)} async-done(((bf16[4,2,256,128]{3,2,1,0:T(8,128)(2,1)}), bf16[4,2,256,128]{3,2,1,0:T(8,128)(2,1)S(1)}, u32[]{:S(2)}, u32[]{:S(2)}) %all-to-all-start.3) | async-done | bytes 524320 | tf_op jit(solution)/shard_map/all_to_all | solution.py:59
  80.2 4.3 %all-to-all-start = ((f32[8,1,4,128,128]{4,3,2,1,0:T(8,128)}), f32[8,1,4,128,128]{4,3,2,1,0:T(8,128)}, u32[]{:S(2)}, u32[]{:S(2)}) async-start(f32[8,1,4,128,128]{4,3,2,1,0:T(8,128)} %select_bitcast_fusion), calls=%async_computation | async-start | bytes 4194304 | tf_op jit(solution)/shard_map/all_to_all | solution.py:42
  87.5 6.2 %fusion.22 = bf16[8,4,256,128]{2,3,1,0:T(8,128)(2,1)} fusion(f32[8,4,256]{2,1,0:T(4,128)S(1)} %copy.146, pred[8,256,256]{2,1,0:T(8,128)(4,1)S(1)} %and_and_fusion, bf16[8,256,4,128]{1,3,2,0:T(8,128)(2,1)} %bitcast.212, bf16[8,256,512]{2,1,0:T(8,128)(2,1)S(1)} %copy-done, bf16[8,256,512]{2,1,0:T(8,128)(2,1)} %param.22), kind=kOutput, calls=%fused_computation.35 | convolution fusion | flops 1085276160 | bytes 8945664 | tf_op jit(solution)/shard_map/rhts,rshd->rthd/dot_general | solution.py:142
  93.7 37.6 %all-to-all-done = f32[8,1,4,128,128]{4,3,2,1,0:T(8,128)} async-done(((f32[8,1,4,128,128]{4,3,2,1,0:T(8,128)}), f32[8,1,4,128,128]{4,3,2,1,0:T(8,128)}, u32[]{:S(2)}, u32[]{:S(2)}) %all-to-all-start) | async-done | bytes 2097184 | tf_op jit(solution)/shard_map/all_to_all | solution.py:42
  131.3 3.5 %all-to-all-start.5 = ((bf16[4,2,256,128]{3,2,1,0:T(8,128)(2,1)}), bf16[4,2,256,128]{3,2,1,0:T(8,128)(2,1)S(1)}, u32[]{:S(2)}, u32[]{:S(2)}) async-start(bf16[4,2,256,128]{3,2,1,0:T(8,128)(2,1)} %bitcast.50), calls=%async_computation.5 | async-start | bytes 1048576 | tf_op jit(solution)/shard_map/all_to_all | solution.py:62
  135.2 3.9 %copy.175 = bf16[8,256,512]{2,1,0:T(8,128)(2,1)} copy(bf16[8,256,512]{1,2,0:T(8,128)(2,1)} %bitcast.214) | data formatting | bytes 4194304
  140.8 3.6 %gather_fusion.2 = f32[8,4,128,128]{3,2,1,0:T(8,128)} fusion(f32[8,4,128,128]{3,2,1,0:T(8,128)} %bitcast.9, s32[1024]{0:T(1024)S(1)} %pad_clamp_fusion.2), kind=kCustom, calls=%fused_computation.2.clone | custom fusion | bytes 4194336 | tf_op jit(solution)/shard_map/jit(_take)/gather | solution.py:32
  144.4 3.2 %broadcast_select_fusion = f32[8,4,128,128]{3,2,1,0:T(8,128)} fusion(f32[8,4,128,128]{3,2,1,0:T(8,128)} %gather_fusion.2, pred[8]{0:T(512)(128)(4,1)S(1)} %copy-done.15), kind=kLoop, calls=%fused_computation.68 | loop fusion | flops 524288 | bytes 4194312 | tf_op jit(solution)/shard_map/jit(_take)/select_n | solution.py:32
  147.6 4.6 %all-to-all-start.1 = ((f32[4,2,4,128,128]{4,3,2,1,0:T(8,128)}), f32[4,2,4,128,128]{4,3,2,1,0:T(8,128)}, u32[]{:S(2)}, u32[]{:S(2)}) async-start(f32[4,2,4,128,128]{4,3,2,1,0:T(8,128)} %bitcast.213), calls=%async_computation.1 | async-start | bytes 4194304 | tf_op jit(solution)/shard_map/all_to_all | solution.py:55
  153.8 1.4 fusion.157
  159.9 40.2 %all-to-all-done.1 = f32[4,2,4,128,128]{4,3,2,1,0:T(8,128)} async-done(((f32[4,2,4,128,128]{4,3,2,1,0:T(8,128)}), f32[4,2,4,128,128]{4,3,2,1,0:T(8,128)}, u32[]{:S(2)}, u32[]{:S(2)}) %all-to-all-start.1) | async-done | bytes 2097184 | tf_op jit(solution)/shard_map/all_to_all | solution.py:55
  200.1 3.6 %gather_fusion.3 = f32[8,4,128,128]{3,2,1,0:T(8,128)} fusion(f32[8,4,128,128]{3,2,1,0:T(8,128)} %bitcast.11, s32[1024]{0:T(1024)S(1)} %pad_clamp_fusion.1), kind=kCustom, calls=%fused_computation.3.clone | custom fusion | bytes 4194336 | tf_op jit(solution)/shard_map/jit(_take)/gather | solution.py:32
  203.6 5.0 %fusion.17 = bf16[8,4,1,128]{3,2,1,0:T(2,128)(2,1)S(1)} fusion(f32[8,4,128]{2,1,0:T(4,128)S(1)} %copy.166, f32[8,4,128]{2,1,0:T(4,128)S(1)} %copy.165, f32[8,4]{1,0:T(8,128)S(1)} %copy.164, f32[8,4,128]{2,1,0:T(4,128)S(1)} %copy.163, f32[8,4,128]{2,1,0:T(4,128)S(1)} %copy.162, f32[8,4]{1,0:T(8,128)S(1)} %copy.161, f32[8,4,128]{2,1,0:T(4,128)S(1)} %copy.160, ...), kind=kOutput, calls=%fused_computation.27 | convolution fusion | flops 13107200 | bytes 2245128 | tf_op jit(solution)/shard_map/rhd,rhde->rhe/dot_general | solution.py:164
  208.7 3.1 %fusion.30 = bf16[8,4,1,128]{3,2,1,0:T(2,128)(2,1)S(1)} fusion(f32[8,4,128]{2,1,0:T(4,128)S(1)} %copy.163, f32[8,4,128]{2,1,0:T(4,128)S(1)} %copy.162, f32[8,4]{1,0:T(8,128)S(1)} %copy.161, f32[8,4,128]{2,1,0:T(4,128)S(1)} %copy.160, f32[8,4,128]{2,1,0:T(4,128)S(1)} %copy.159, f32[8,4]{1,0:T(8,128)S(1)} %copy.158, ...), kind=kOutput, calls=%fused_computation.39 | convolution fusion | flops 11534336 | bytes 2212232 | tf_op jit(solution)/shard_map/rhd,rhde->rhe/dot_general | solution.py:164
  211.7 2.5 fusion.29
  214.2 1.6 fusion.104
  215.9 4.9 %fusion.76 = f32[32,6144]{1,0:T(8,128)} fusion(bf16[512,6144]{1,0:T(8,128)(2,1)} %param.30, bf16[1,8,512]{2,1,0:T(8,128)(2,1)S(1)} %bitcast.218, bf16[1,8,512]{2,1,0:T(8,128)(2,1)S(1)} %bitcast.219, bf16[1,8,512]{2,1,0:T(8,128)(2,1)S(1)} %bitcast.220, bf16[1,8,512]{2,1,0:T(8,128)(2,1)S(1)} %convert_element_type.277), kind=kOutput, calls=%fused_computation.127 | convolution fusion | flops 201375744 | bytes 7110656 | tf_op jit(solution)/shard_map/dot_general | solution.py:194
  222.0 64.8 %all-reduce.2.cloned.1.call-done = f32[32,6144]{1,0:T(8,128)} async-done(((f32[32,6144]{1,0:T(8,128)}), f32[32,6144]{1,0:T(8,128)}) %all-reduce.2.cloned.1.call-update) | async-done | bytes 786448 | tf_op jit(solution)/shard_map/psum | solution.py:195
  288.2 2.0 fusion.65
  (157 shorter events, 19.6 us)
Async XLA Ops:
  7.2 34.6 %copy-start = (bf16[8,256,512]{2,1,0:T(8,128)(2,1)S(1)}, bf16[8,256,512]{2,1,0:T(8,128)(2,1)}, u32[]{:S(2)}) copy-start(bf16[8,256,512]{2,1,0:T(8,128)(2,1)} %param.24) | copy-start | bytes 6291460
  10.3 14.3 %copy-start.13 = (s32[256]{0:T(256)S(1)}, s32[256]{0:T(256)}, u32[]{:S(2)}) copy-start(s32[256]{0:T(256)} %param.27) | copy-start | bytes 3076
  10.4 14.4 %copy-start.1 = (s32[256]{0:T(256)S(1)}, s32[256]{0:T(256)}, u32[]{:S(2)}) copy-start(s32[256]{0:T(256)} %param.26) | copy-start | bytes 3076
  10.4 14.5 %copy-start.9 = (f32[8,256,4]{1,2,0:T(4,128)S(1)}, f32[8,256,4]{1,2,0:T(4,128)}, u32[]{:S(2)}) copy-start(f32[8,256,4]{1,2,0:T(4,128)} %param.25) | copy-start | bytes 98308
  13.2 23.1 %all-to-all-start.2 = ((bf16[8,1,256,128]{3,2,1,0:T(8,128)(2,1)}), bf16[8,1,256,128]{3,2,1,0:T(8,128)(2,1)S(1)}, u32[]{:S(2)}, u32[]{:S(2)}) async-start(bf16[8,1,256,128]{3,2,1,0:T(8,128)(2,1)} %get-tuple-element.60), calls=%async_computation.2 | async-start | bytes 1048576 | tf_op jit(solution)/shard_map/all_to_all | solution.py:46
  36.3 16.7 %all-to-all-start.4 = ((bf16[8,1,256,128]{3,2,1,0:T(8,128)(2,1)}), bf16[8,1,256,128]{3,2,1,0:T(8,128)(2,1)}, u32[]{:S(2)}, u32[]{:S(2)}) async-start(bf16[8,1,256,128]{3,2,1,0:T(8,128)(2,1)} %get-tuple-element.59), calls=%async_computation.4 | async-start | bytes 1048576 | tf_op jit(solution)/shard_map/all_to_all | solution.py:47
  41.7 12.9 %copy-start.14 = (pred[8]{0:T(512)(128)(4,1)}, pred[8]{0:T(512)(128)(4,1)S(1)}, u32[]{:S(2)}) copy-start(pred[8]{0:T(512)(128)(4,1)S(1)} %compare_and_fusion.1) | copy-start | bytes 28
  55.8 24.5 %all-to-all-start.3 = ((bf16[4,2,256,128]{3,2,1,0:T(8,128)(2,1)}), bf16[4,2,256,128]{3,2,1,0:T(8,128)(2,1)S(1)}, u32[]{:S(2)}, u32[]{:S(2)}) async-start(bf16[4,2,256,128]{3,2,1,0:T(8,128)(2,1)} %bitcast.45), calls=%async_computation.3 | async-start | bytes 1048576 | tf_op jit(solution)/shard_map/all_to_all | solution.py:59
  74.0 12.6 %copy-start.12 = (f32[4,8,4]{1,2,0:T(4,128)S(1)}, f32[4,8,4]{1,2,0:T(4,128)}, u32[]{:S(2)}) copy-start(f32[4,8,4]{1,2,0:T(4,128)} %param.36) | copy-start | bytes 1540
  74.0 12.6 %copy-start.10 = (bf16[4,8,512]{2,1,0:T(8,128)(2,1)S(1)}, bf16[4,8,512]{2,1,0:T(8,128)(2,1)}, u32[]{:S(2)}) copy-start(bf16[4,8,512]{2,1,0:T(8,128)(2,1)} %param.33) | copy-start | bytes 98308
  74.0 12.6 %copy-start.6 = (bf16[4,8,1024]{2,1,0:T(8,128)(2,1)S(1)}, bf16[4,8,1024]{2,1,0:T(8,128)(2,1)}, u32[]{:S(2)}) copy-start(bf16[4,8,1024]{2,1,0:T(8,128)(2,1)} %param.37) | copy-start | bytes 196612
  74.0 12.6 %copy-start.17 = (bf16[4,8,128]{2,1,0:T(8,128)(2,1)S(1)}, bf16[4,8,128]{2,1,0:T(8,128)(2,1)}, u32[]{:S(2)}) copy-start(bf16[4,8,128]{2,1,0:T(8,128)(2,1)} %param.38) | copy-start | bytes 24580
  74.0 12.9 %copy-start.7 = (bf16[4,8,512]{2,1,0:T(8,128)(2,1)S(1)}, bf16[4,8,512]{2,1,0:T(8,128)(2,1)}, u32[]{:S(2)}) copy-start(bf16[4,8,512]{2,1,0:T(8,128)(2,1)} %param.34) | copy-start | bytes 98308
  74.0 12.9 %copy-start.8 = (bf16[4,8,512]{2,1,0:T(8,128)(2,1)S(1)}, bf16[4,8,512]{2,1,0:T(8,128)(2,1)}, u32[]{:S(2)}) copy-start(bf16[4,8,512]{2,1,0:T(8,128)(2,1)} %param.35) | copy-start | bytes 98308
  80.2 51.1 %all-to-all-start = ((f32[8,1,4,128,128]{4,3,2,1,0:T(8,128)}), f32[8,1,4,128,128]{4,3,2,1,0:T(8,128)}, u32[]{:S(2)}, u32[]{:S(2)}) async-start(f32[8,1,4,128,128]{4,3,2,1,0:T(8,128)} %select_bitcast_fusion), calls=%async_computation | async-start | bytes 4194304 | tf_op jit(solution)/shard_map/all_to_all | solution.py:42
  131.3 16.3 %all-to-all-start.5 = ((bf16[4,2,256,128]{3,2,1,0:T(8,128)(2,1)}), bf16[4,2,256,128]{3,2,1,0:T(8,128)(2,1)S(1)}, u32[]{:S(2)}, u32[]{:S(2)}) async-start(bf16[4,2,256,128]{3,2,1,0:T(8,128)(2,1)} %bitcast.50), calls=%async_computation.5 | async-start | bytes 1048576 | tf_op jit(solution)/shard_map/all_to_all | solution.py:62
  135.2 3.9 %copy-start.18 = (bf16[4,8,128]{2,1,0:T(8,128)(2,1)S(1)}, bf16[4,8,128]{2,1,0:T(8,128)(2,1)}, u32[]{:S(2)}) copy-start(bf16[4,8,128]{2,1,0:T(8,128)(2,1)} %param.38) | copy-start | bytes 24580
  140.8 3.6 %copy-start.15 = (pred[8]{0:T(512)(128)(4,1)S(1)}, pred[8]{0:T(512)(128)(4,1)}, u32[]{:S(2)}) copy-start(pred[8]{0:T(512)(128)(4,1)} %copy-done.14) | copy-start | bytes 28
  147.6 4.8 %copy-start.4 = (bf16[8,256,128]{2,1,0:T(8,128)(2,1)S(1)}, bf16[8,256,128]{2,1,0:T(8,128)(2,1)}, u32[]{:S(2)}) copy-start(bf16[8,256,128]{2,1,0:T(8,128)(2,1)} %gather_fusion.6) | copy-start | bytes 1572868
  147.6 4.8 %copy-start.16 = (pred[8,256]{1,0:T(8,128)(4,1)S(1)}, pred[8,256]{1,0:T(8,128)(4,1)}, u32[]{:S(2)}) copy-start(pred[8,256]{1,0:T(8,128)(4,1)} %iota_compare_fusion.2) | copy-start | bytes 6148
  147.6 4.8 %copy-start.20 = (pred[8]{0:T(512)(128)(4,1)S(1)}, pred[8]{0:T(512)(128)(4,1)}, u32[]{:S(2)}) copy-start(pred[8]{0:T(512)(128)(4,1)} %compare_and_fusion) | copy-start | bytes 28
  147.6 52.4 %all-to-all-start.1 = ((f32[4,2,4,128,128]{4,3,2,1,0:T(8,128)}), f32[4,2,4,128,128]{4,3,2,1,0:T(8,128)}, u32[]{:S(2)}, u32[]{:S(2)}) async-start(f32[4,2,4,128,128]{4,3,2,1,0:T(8,128)} %bitcast.213), calls=%async_computation.1 | async-start | bytes 4194304 | tf_op jit(solution)/shard_map/all_to_all | solution.py:55
  152.3 134.5 %all-reduce.2.cloned.1.call-start = ((), (), s32[]{:S(2)}) async-start(), calls=%async_computation.6 | async-start | bytes 1572864 | tf_op jit(solution)/shard_map/psum | solution.py:195
  152.9 5.5 %copy-start.21 = (pred[8]{0:T(512)(128)(4,1)S(1)}, pred[8]{0:T(512)(128)(4,1)}, u32[]{:S(2)}) copy-start(pred[8]{0:T(512)(128)(4,1)} %compare_and_fusion) | copy-start | bytes 28
  153.6 3.6 %copy-start.5 = (bf16[8,256,128]{2,1,0:T(8,128)(2,1)S(1)}, bf16[8,256,128]{2,1,0:T(8,128)(2,1)}, u32[]{:S(2)}) copy-start(bf16[8,256,128]{2,1,0:T(8,128)(2,1)} %gather_fusion.6) | copy-start | bytes 1572868
  153.8 4.9 %copy-start.19 = (bf16[4,8,128]{2,1,0:T(8,128)(2,1)S(1)}, bf16[4,8,128]{2,1,0:T(8,128)(2,1)}, u32[]{:S(2)}) copy-start(bf16[4,8,128]{2,1,0:T(8,128)(2,1)} %param.39) | copy-start | bytes 24580
  203.6 5.0 %copy-start.2 = (f32[8,4,128,128]{3,2,1,0:T(8,128)S(1)}, f32[8,4,128,128]{3,2,1,0:T(8,128)}, u32[]{:S(2)}) copy-start(f32[8,4,128,128]{3,2,1,0:T(8,128)} %gather_fusion.3) | copy-start | bytes 6291460
  215.9 70.9 %copy-start.3 = (bf16[4,8,6144]{2,1,0:T(8,128)(2,1)S(1)}, bf16[4,8,6144]{2,1,0:T(8,128)(2,1)}, u32[]{:S(2)}) copy-start(bf16[4,8,6144]{2,1,0:T(8,128)(2,1)} %param.32) | copy-start | bytes 1179652
  220.8 67.3 %copy-start.11 = (f32[6144]{0:T(1024)S(1)}, f32[6144]{0:T(1024)}, u32[]{:S(2)}) copy-start(f32[6144]{0:T(1024)} %param.31) | copy-start | bytes 73732
Sparse Core Ops, SparseCore 0:
  221.0 65.7 all-reduce.1
where the time goes:
time: 299 us; the launch traced here: 297 us
  waiting for transfers between devices  158 us (53%)
  starting transfers between devices  40.6 us (14%)
  matrix products  35.3 us (12%)
  local copies, waits for them, and re-layouts  28 us (9%)
  other arithmetic  20.6 us (7%)
  between operations  14.7 us (5%)
    psum x1, waiting for transfers between devices, on_device(): summed = lax.psum(projected, 'tp')  64.8 us
    all_to_all x1, waiting for transfers between devices, section_leg(): lax.all_to_all(blocked(states, count), 'section', split_axis=0, concat_ax...  40.2 us
    all_to_all x1, waiting for transfers between devices, rep_leg(): lax.all_to_all(blocked(states, count), 'rep', split_axis=0, concat_axis=0...  37.6 us
    gather x9, local copies, waits for them, and re-layouts, reorder(): return tuple((jnp.take(piece, index, axis=0) for piece in parts))  18.5 us
    dot_general x4, matrix products, on_device(): linear = jnp.einsum('rhd,rhde->rhe', query_now, carried, precision=HIGHEST)  12.2 us
    all_to_all x1, starting transfers between devices, rep_leg(): lax.all_to_all(blocked(keys_part, count), 'rep', split_axis=0, concat_axi...  11.5 us
    all_to_all x1, starting transfers between devices, section_leg(): lax.all_to_all(blocked(keys_part, count), 'section', split_axis=0, concat...  11.1 us
    dot_general x1, matrix products, on_device(): jnp.einsum('rhts,rshd->rthd', weights, values_four, preferred_element_typ...  6.25 us
  transfers between devices with their start and end apart: 7, of which 6 were waited for; matrix products, arithmetic and copies ran while one was open for 17% of the time, Pallas kernels for 0%

commit v1 on v0

v1 whole, which is shorter than its diff:
```python
import functools
import math

import jax
import jax.numpy as jnp
from jax import lax
from jax.experimental import pallas as pl
from jax.experimental.pallas import tpu as pltpu
from jax.sharding import PartitionSpec as P

MESH = pl.DeviceIdType.MESH
F32 = jnp.float32
BF16 = jnp.bfloat16
LOG2E = 1.0 / math.log(2.0)
LANES = 128


def iota(shape, axis):
    return lax.broadcasted_iota(jnp.int32, shape, axis)


def dot(a, b):
    return jnp.dot(a, b, preferred_element_type=F32)


def dot_nt(a, b, precision=None):
    return lax.dot_general(
        a, b, (((1,), (1,)), ((), ())), preferred_element_type=F32, precision=precision
    )


def one_hot(mask):
    return jnp.where(mask, 1.0, 0.0).astype(BF16)


def split_two(x):
    high = x.astype(BF16)
    return high, (x - high.astype(F32)).astype(BF16)


def body(
    dims,
    pq_hbm,
    pk_hbm,
    pv_hbm,
    gate_hbm,
    len_hbm,
    dg_hbm,
    dgv_hbm,
    ck_hbm,
    cv_hbm,
    w_hbm,
    gain_hbm,
    si_hbm,
    sq_hbm,
    sk_hbm,
    sv_hbm,
    sg_hbm,
    fq_hbm,
    fk_hbm,
    fv_hbm,
    po_hbm,
    do_hbm,
    so_hbm,
    pq,
    pk,
    pv,
    gate,
    len_s,
    dg_s,
    dgv,
    ck,
    cv,
    w,
    gain,
    si,
    sq,
    sk,
    sv,
    sg,
    fq,
    fk,
    fv,
    po,
    so,
    rowf,
    decf,
    colm,
    own,
    gamma,
    sel_lin,
    sel_soft,
    send_q,
    recv_q,
    res_q,
    send_r,
    recv_r,
    send_s,
    recv_s,
    res_s,
    send_t,
    recv_t,
    part_f,
    part_b,
    recv_p,
    ss_send,
    ss_recv,
    ag,
    in_sem,
    out_sem,
    q_sem,
    r_sem,
    s_sem,
    t_sem,
    rs_send,
    rs_recv,
    sib_sem,
    ag_send,
    ag_recv,
):
    sections, reps, tps, held, length, heads, steps, q_heads, model = dims
    groups = sections * reps
    total = groups * held
    me_s = lax.axis_index("section")
    me_r = lax.axis_index("rep")
    me_p = lax.axis_index("tp")
    me_g = me_s * reps + me_r
    first = me_g * held
    half = model // 2
    per_owner = steps * 2 // tps
    me_y = me_p // 2
    me_c = me_p % 2
    lin_rows = heads * steps
    soft_rows = q_heads * steps

    barrier = pltpu.get_barrier_semaphore()

    def greet(off, carry):
        peer = lax.rem(me_g + off, groups)
        pl.semaphore_signal(
            barrier, inc=1, device_id=(peer // reps, lax.rem(peer, reps), me_p), device_id_type=MESH
        )
        return carry

    lax.fori_loop(1, groups, greet, 0)

    def greet_tp(off, carry):
        pl.semaphore_signal(
            barrier,
            inc=1,
            device_id=(me_s, me_r, lax.rem(me_p + off, tps)),
            device_id_type=MESH,
        )
        return carry

    lax.fori_loop(1, tps, greet_tp, 0)

    y0 = me_y * per_owner
    col0 = pl.multiple_of(me_c * half, LANES)
    loads = {}
    for place, (name, src, dst) in enumerate(
        (
            ("dgv", dgv_hbm, dgv),
            ("sq", sq_hbm, sq),
            ("dg", dg_hbm, dg_s),
            ("len", len_hbm, len_s),
            ("gate", gate_hbm, gate),
            ("pk", pk_hbm, pk),
            ("pv", pv_hbm, pv),
            ("pq", pq_hbm, pq),
            ("fq", fq_hbm, fq),
            ("fk", fk_hbm, fk),
            ("fv", fv_hbm, fv),
            ("sk", sk_hbm, sk),
            ("sv", sv_hbm, sv),
            ("sg", sg_hbm, sg),
            ("w", w_hbm, w),
            ("ck", ck_hbm, ck),
            ("cv", cv_hbm, cv),
            ("si", si_hbm.at[pl.ds(y0, per_owner), :, pl.ds(col0, half)], si),
            ("gain", gain_hbm.at[:, pl.ds(col0, half)], gain),
        )
    ):
        loads[name] = pltpu.make_async_copy(src, dst, in_sem.at[place])
        loads[name].start()

    loads["dgv"].wait()
    mine = dgv[...] == me_g
    mine_rows = jnp.broadcast_to(one_hot(mine), (16, total))
    before = one_hot(iota((total, total), 0) < iota((total, total), 1))
    rank = dot(mine_rows, before)[0:1]
    slot_row = lax.rem(iota((soft_rows * held, total), 0), held).astype(F32)
    slot_of = one_hot(jnp.where(mine, rank, -1.0) == slot_row)
    slot_lin = slot_of[: lin_rows * held]

    def rep_rows(rows_each):
        shape = (rows_each * reps, total)
        source_rep = lax.rem(iota(shape, 1) // held, reps)
        return one_hot(iota(shape, 0) // rows_each == source_rep)

    def spread(rows_each, slots):
        picked = dot_nt(rep_rows(rows_each), slots)
        same = lax.rem(iota(picked.shape, 0), rows_each) == iota(picked.shape, 1) // held
        return jnp.where(same, picked, 0.0).astype(BF16)

    def by_row(ref, count):
        pieces = [
            ref[i, :, a * LANES : (a + 1) * LANES].astype(F32)
            for a in range(count)
            for i in range(steps)
        ]
        return jnp.concatenate(pieces, axis=0).astype(BF16)

    loads["sq"].wait()
    spread_lin = spread(lin_rows, slot_lin)
    blocks = dot(spread_lin, by_row(sq, heads)).astype(BF16)
    send_q[...] = blocks.reshape(reps, lin_rows, LANES)

    pl.semaphore_wait(barrier, groups - 1 + tps - 1)

    def to_groups(src, dst, sems):
        def one(off, carry):
            peer = lax.rem(me_g + off, groups)
            peer_r = lax.rem(peer, reps)
            pltpu.make_async_remote_copy(
                src_ref=src.at[peer_r],
                dst_ref=dst.at[me_g],
                send_sem=sems.at[0],
                recv_sem=sems.at[1],
                device_id=(peer // reps, peer_r, me_p),
                device_id_type=MESH,
            ).start()
            return carry

        lax.fori_loop(1, groups, one, 0)
        dst[me_g] = src[me_r]

    def all_bytes(dst, sem):
        view = dst.at[pl.ds(0, groups - 1)]
        pltpu.make_async_copy(view, view, sem).wait()

    to_groups(send_q, recv_q, q_sem)

    loads["dg"].wait()
    loads["len"].wait()
    loads["gate"].wait()
    count = held * heads
    shape = (count, length)
    own_len = [len_s[first + k] for k in range(held)]
    logs = jnp.log(jnp.concatenate([gate[k] for k in range(held)], axis=0))
    len_rows = jnp.zeros(shape, jnp.int32)
    for k in range(held):
        len_rows = jnp.where(iota(shape, 0) // heads == k, own_len[k], len_rows)
    inside = iota(shape, 1) < len_rows
    logs = jnp.where(inside, logs, 0.0)
    p1, rest = split_two(logs)
    rest = logs - p1.astype(F32)
    p2, p3 = split_two(rest)
    upto = one_hot(iota((length, length), 0) <= iota((length, length), 1))
    upto_t = one_hot(iota((length, length), 1) <= iota((length, length), 0))
    cum_rows = (dot(p1, upto) + dot(p2, upto) + dot(p3, upto)) * LOG2E
    cum_cols = (dot_nt(upto_t, p1) + dot_nt(upto_t, p2) + dot_nt(upto_t, p3)) * LOG2E
    decays = jnp.where(inside, jnp.exp2(cum_rows[:, length - 1 :] - cum_rows), 0.0)
    shape = (length, count)
    len_cols = jnp.zeros(shape, jnp.int32)
    for k in range(held):
        len_cols = jnp.where(iota(shape, 1) // heads == k, own_len[k], len_cols)
    cum_cols = jnp.where(iota(shape, 0) < len_cols, cum_cols, -jnp.inf)
    for k in range(held):
        rows = slice(k * heads, (k + 1) * heads)
        rowf[k] = cum_rows[rows]
        decf[k] = decays[rows]
        colm[k] = cum_cols[:, rows]

    loads["pk"].wait()
    loads["pv"].wait()
    loads["pq"].wait()
    mid = length // 2

    def prompt(k, carry):
        causal = iota((mid, mid), 0) >= iota((mid, mid), 1)
        for h in range(heads):
            lanes = slice(h * LANES, (h + 1) * LANES)
            scores = dot_nt(pq[k, :, lanes], pk[k, :, lanes])
            row = rowf[k, h : h + 1, :]
            col = colm[k, :, h : h + 1]
            values = pv[k, :, lanes]
            gap = jnp.where(causal, col[:mid] - row[:, :mid], -jnp.inf)
            top = (jnp.exp2(gap) * scores[:mid, :mid]).astype(BF16)
            low_left = (jnp.exp2(col[mid:] - row[:, :mid]) * scores[mid:, :mid]).astype(BF16)
            gap = jnp.where(causal, col[mid:] - row[:, mid:], -jnp.inf)
            low_right = (jnp.exp2(gap) * scores[mid:, mid:]).astype(BF16)
            low = jnp.concatenate([low_left, low_right], axis=1)
            po[k, :mid, lanes] = dot(top, values[:mid]).astype(BF16)
            po[k, mid:, lanes] = dot(low, values).astype(BF16)
        pltpu.make_async_copy(po.at[k], po_hbm.at[k], out_sem.at[k]).start()
        return carry

    marks = [0, held // 4, held // 2 + 1, held // 2 + 2, held]
    lax.fori_loop(marks[0], marks[1], prompt, 0)

    for name in ("fq", "fk", "fv", "sk", "sv", "sg"):
        loads[name].wait()
    soft_blocks = dot(spread(soft_rows, slot_of), by_row(fq, q_heads)).astype(BF16)
    send_s[:, :soft_rows, :] = soft_blocks.reshape(reps, soft_rows, LANES)
    fresh = jnp.concatenate([by_row(fk, 1).astype(F32), by_row(fv, 1).astype(F32)], axis=0)
    fresh_spread = spread_lin[:, : 2 * steps * held]
    fresh_blocks = dot(fresh_spread, fresh.astype(BF16)).astype(BF16)
    send_s[:, soft_rows:, :] = fresh_blocks.reshape(reps, lin_rows, LANES)

    target_rep = [lax.rem(dg_s[first + k], reps) for k in range(held)]
    bound_for = []
    for r in range(reps):
        found = jnp.int32(0)
        for k in range(held):
            found = jnp.where(target_rep[k] == r, k, found)
        bound_for.append(found)
    all_bytes(recv_q, q_sem.at[1])
    head_of_row = iota((lin_rows, length), 0) // steps
    for k in range(held):
        asked = recv_q[dg_s[first + k]]
        result = jnp.zeros((2 * lin_rows, LANES), F32)
        for h in range(heads):
            lanes = slice(h * LANES, (h + 1) * LANES)
            weights = dot_nt(asked, pk[k, :, lanes]) * decf[k, h : h + 1, :]
            high, low = split_two(jnp.where(head_of_row == h, weights, 0.0))
            result = result + dot(jnp.concatenate([high, low], axis=0), pv[k, :, lanes])
        res_q[k] = (result[:lin_rows] + result[lin_rows:]).astype(BF16)
    for r in range(reps):
        send_r[r] = res_q[bound_for[r]]
    to_groups(send_r, recv_r, r_sem)
    to_groups(send_s, recv_s, s_sem)

    eye = jnp.where(iota((held, held), 0) == iota((held, held), 1), 1.0, 0.0)
    gates = [dot_nt(eye, sg[i], lax.Precision.HIGHEST) for i in range(steps)]
    for h in range(heads):
        lanes = slice(h * LANES, (h + 1) * LANES)
        running = jnp.ones((held, 1), F32)
        for i in range(steps):
            running = running * gates[i][:, h : h + 1]
            gamma[i, :, lanes] = jnp.broadcast_to(running, (held, LANES))
            query = sq[i, :, lanes].astype(F32)
            added = jnp.zeros((held, LANES), F32)
            since = jnp.ones((held, 1), F32)
            for u in range(i, -1, -1):
                pair = jnp.sum(query * sk[u, :, lanes].astype(F32), axis=1, keepdims=True)
                added = added + (since * pair) * sv[u, :, lanes].astype(F32)
                since = since * gates[u][:, h : h + 1]
            own[i, :, lanes] = added

    def pick(rows_each, slots):
        shape = (total, rows_each * groups)
        source = one_hot(iota(shape, 0) // held == iota(shape, 1) // rows_each)
        picked = dot(slots, source)
        same = iota(picked.shape, 0) // held == lax.rem(iota(picked.shape, 1), rows_each)
        return jnp.where(same, picked, 0.0).astype(BF16)

    sel_lin[...] = pick(lin_rows, slot_lin)
    lax.fori_loop(marks[1], marks[2], prompt, 0)

    loads["w"].wait()
    all_bytes(recv_r, r_sem.at[1])
    carried = dot(sel_lin[...], recv_r[...].reshape(groups * lin_rows, LANES))
    hidden = []
    for i in range(steps):
        across = []
        for h in range(heads):
            lanes = slice(h * LANES, (h + 1) * LANES)
            rows = slice((h * steps + i) * held, (h * steps + i + 1) * held)
            across.append(gamma[i, :, lanes] * carried[rows] + own[i, :, lanes])
        hidden.append(jnp.concatenate(across, axis=1))
    hidden = jnp.concatenate(hidden, axis=0).astype(BF16)
    pieces = 4
    wide = model // pieces
    owners = tps // 2

    def piece_copy(c, owner, source):
        return pltpu.make_async_remote_copy(
            src_ref=part_b.at[pl.ds(owner * per_owner, per_owner), :, c * wide : (c + 1) * wide],
            dst_ref=recv_p.at[source, c % 2],
            send_sem=rs_send.at[owner, c],
            recv_sem=rs_recv.at[source, c % 2],
            device_id=(me_s, me_r, owner * 2 + c // 2),
            device_id_type=MESH,
        )

    for c in range(pieces):
        cols = slice(c * wide, (c + 1) * wide)
        partial = dot(hidden, w[:, cols])
        for i in range(steps):
            rows = partial[i * held : (i + 1) * held]
            part_f[i, :, cols] = rows
            part_b[i, :, cols] = rows.astype(BF16)

        for off in range(owners):
            owner = lax.rem(me_y + 1 + off, owners)

            @pl.when((owner != me_y) | (me_c != c // 2))
            def _():
                piece_copy(c, owner, me_p).start()

    loads["ck"].wait()
    loads["cv"].wait()
    all_bytes(recv_s, s_sem.at[1])
    scale = LOG2E / math.sqrt(LANES)

    def soft(k, carry):
        block = recv_s[dg_s[first + k]]
        asked = block[:soft_rows]
        fresh_rows = block[soft_rows:]
        scores = dot_nt(asked, ck[k]) * scale
        scores = jnp.where(iota(scores.shape, 1) < len_s[first + k], scores, -jnp.inf)
        news = dot_nt(asked, fresh_rows) * scale
        lane = iota(news.shape, 1)
        seen = (lane < steps) & (lane <= lax.rem(iota(news.shape, 0), steps))
        news = jnp.where(seen, news, -jnp.inf)
        peak = jnp.maximum(
            jnp.max(scores, axis=1, keepdims=True), jnp.max(news, axis=1, keepdims=True)
        )
        scores = jnp.exp2(scores - peak)
        news = jnp.exp2(news - peak)
        bottom = jnp.sum(scores, axis=1, keepdims=True) + jnp.sum(news, axis=1, keepdims=True)
        probs = (scores / bottom).astype(BF16)
        fresh_probs = (news / bottom).astype(BF16).astype(F32)
        fresh_values = fresh_rows.astype(F32)
        mixed = dot(probs, cv[k])
        for u in range(steps):
            mixed = mixed + fresh_probs[:, u : u + 1] * fresh_values[steps + u : steps + u + 1]
        res_s[k] = mixed.astype(BF16)
        return carry

    lax.fori_loop(0, held, soft, 0)
    for r in range(reps):
        send_t[r] = res_s[bound_for[r]]
    to_groups(send_t, recv_t, t_sem)
    sel_soft[...] = pick(soft_rows, slot_of)

    loads["si"].wait()
    loads["gain"].wait()
    summed = []
    for part in range(2):
        cols = pl.ds(pl.multiple_of(me_c * half + part * wide, LANES), wide)
        here = slice(part * wide, (part + 1) * wide)
        value = part_f[pl.ds(y0, per_owner), :, cols] + si[:, :, here].astype(F32)
        for off in range(1, tps):
            source = lax.rem(me_p + off, tps)
            pltpu.make_async_copy(
                recv_p.at[source, part], recv_p.at[source, part], rs_recv.at[source, part]
            ).wait()
            value = value + recv_p[source, part].astype(F32)
        summed.append(value)
    square = jnp.sum(summed[0] * summed[0], axis=2, keepdims=True)
    square = square + jnp.sum(summed[1] * summed[1], axis=2, keepdims=True)
    ss_send[...] = jnp.broadcast_to(square, ss_send.shape)
    sibling = pltpu.make_async_remote_copy(
        src_ref=ss_send,
        dst_ref=ss_recv,
        send_sem=sib_sem.at[0],
        recv_sem=sib_sem.at[1],
        device_id=(me_s, me_r, me_p + 1 - 2 * me_c),
        device_id_type=MESH,
    )
    sibling.start()
    sibling.wait()
    mean = (square + ss_recv[:, :, 0:1]) / model
    spread_of = jnp.sqrt(mean + 1e-06)
    for part in range(2):
        here = slice(part * wide, (part + 1) * wide)
        gains = gain[:, here].reshape(1, 1, wide)
        ag[:, :, here] = (summed[part] / spread_of * gains).astype(BF16)
    place = do_hbm.at[pl.ds(y0, per_owner), :, pl.ds(col0, half)]
    mine_out = pltpu.make_async_copy(ag, place, out_sem.at[held])
    mine_out.start()

    def gather_copy(peer):
        return pltpu.make_async_remote_copy(
            src_ref=ag,
            dst_ref=place,
            send_sem=ag_send.at[peer],
            recv_sem=ag_recv.at[me_p],
            device_id=(me_s, me_r, peer),
            device_id_type=MESH,
        )

    for off in range(1, tps):
        gather_copy(lax.rem(me_p + off, tps)).start()

    lax.fori_loop(marks[2], marks[4], prompt, 0)

    all_bytes(recv_t, t_sem.at[1])
    placed = dot(sel_soft[...], recv_t[...].reshape(groups * soft_rows, LANES))
    for a in range(q_heads):
        for i in range(steps):
            rows = slice((a * steps + i) * held, (a * steps + i + 1) * held)
            so[i, :, a * LANES : (a + 1) * LANES] = placed[rows].astype(BF16)
    soft_out = pltpu.make_async_copy(so, so_hbm, out_sem.at[held + 1])
    soft_out.start()

    all_bytes(recv_q, q_sem.at[0])
    all_bytes(recv_r, r_sem.at[0])
    all_bytes(recv_s, s_sem.at[0])
    all_bytes(recv_t, t_sem.at[0])
    for c in range(pieces):
        for off in range(owners):
            owner = lax.rem(me_y + 1 + off, owners)

            @pl.when((owner != me_y) | (me_c != c // 2))
            def _():
                piece_copy(c, owner, me_p).wait_send()

    for k in range(held):
        pltpu.make_async_copy(po.at[k], po_hbm.at[k], out_sem.at[k]).wait()
    soft_out.wait()
    mine_out.wait()
    for off in range(1, tps):
        peer = lax.rem(me_p + off, tps)
        gather_copy(peer).wait_send()
        pltpu.make_async_copy(ag, ag, ag_recv.at[peer]).wait()


def on_device(
    prefill_query,
    prefill_key,
    prefill_value,
    prefill_gate,
    lengths,
    decode_group,
    cache_keys,
    cache_values,
    out_weight,
    norm_gain,
    step_input,
    step_query,
    step_key,
    step_value,
    step_gate,
    soft_query,
    soft_new_key,
    soft_new_value,
):
    sections, reps, tps = (lax.axis_size(name) for name in ("section", "rep", "tp"))
    held, length, heads = prefill_gate.shape
    steps = step_query.shape[0]
    q_heads = soft_query.shape[2] // LANES
    model = out_weight.shape[1]
    groups = sections * reps
    width = heads * LANES
    half = model // 2
    per_owner = steps * 2 // tps
    lin_rows = heads * steps
    soft_rows = q_heads * steps
    total = groups * held
    dims = (sections, reps, tps, held, length, heads, steps, q_heads, model)
    operands = (
        prefill_query,
        prefill_key,
        prefill_value,
        jnp.transpose(prefill_gate, (0, 2, 1)),
        lengths,
        decode_group,
        decode_group.reshape(1, total),
        cache_keys,
        cache_values,
        out_weight,
        norm_gain.reshape(1, model),
        step_input,
        step_query,
        step_key,
        step_value,
        jnp.transpose(step_gate, (0, 2, 1)),
        soft_query,
        soft_new_key,
        soft_new_value,
    )
    vmem = pltpu.VMEM
    dma = pltpu.SemaphoreType.DMA
    scratch = [
        vmem((held, length, width), BF16),
        vmem((held, length, width), BF16),
        vmem((held, length, width), BF16),
        vmem((held, heads, length), F32),
        pltpu.SMEM((total,), jnp.int32),
        pltpu.SMEM((total,), jnp.int32),
        vmem((1, total), jnp.int32),
        vmem((held, length, LANES), BF16),
        vmem((held, length, LANES), BF16),
        vmem((width, model), BF16),
        vmem((1, half), F32),
        vmem((per_owner, held, half), BF16),
        vmem((steps, held, width), BF16),
        vmem((steps, held, width), BF16),
        vmem((steps, held, width), BF16),
        vmem((steps, heads, held), F32),
        vmem((steps, held, q_heads * LANES), BF16),
        vmem((steps, held, LANES), BF16),
        vmem((steps, held, LANES), BF16),
        vmem((held, length, width), BF16),
        vmem((steps, held, q_heads * LANES), BF16),
        vmem((held, heads, length), F32),
        vmem((held, heads, length), F32),
        vmem((held, length, heads), F32),
        vmem((steps, held, width), F32),
        vmem((steps, held, width), F32),
        vmem((lin_rows * held, lin_rows * groups), BF16),
        vmem((soft_rows * held, soft_rows * groups), BF16),
        vmem((reps, lin_rows, LANES), BF16),
        vmem((groups, lin_rows, LANES), BF16),
        vmem((held, lin_rows, LANES), BF16),
        vmem((reps, lin_rows, LANES), BF16),
        vmem((groups, lin_rows, LANES), BF16),
        vmem((reps, soft_rows + lin_rows, LANES), BF16),
        vmem((groups, soft_rows + lin_rows, LANES), BF16),
        vmem((held, soft_rows, LANES), BF16),
        vmem((reps, soft_rows, LANES), BF16),
        vmem((groups, soft_rows, LANES), BF16),
        vmem((steps, held, model), F32),
        vmem((steps, held, model), BF16),
        vmem((tps, 2, per_owner, held, half // 2), BF16),
        vmem((per_owner, held, LANES), F32),
        vmem((per_owner, held, LANES), F32),
        vmem((per_owner, held, half), BF16),
        dma((19,)),
        dma((held + 2,)),
        dma((2,)),
        dma((2,)),
        dma((2,)),
        dma((2,)),
        dma((tps // 2, 4)),
        dma((tps, 2)),
        dma((2,)),
        dma((tps,)),
        dma((tps,)),
    ]
    anywhere = pl.BlockSpec(memory_space=pl.ANY)
    return pl.pallas_call(
        functools.partial(body, dims),
        out_shape=(
            jax.ShapeDtypeStruct((held, length, width), BF16),
            jax.ShapeDtypeStruct((steps, held, model), BF16),
            jax.ShapeDtypeStruct((steps, held, q_heads * LANES), BF16),
        ),
        in_specs=[anywhere] * len(operands),
        out_specs=(anywhere,) * 3,
        scratch_shapes=scratch,
        compiler_params=pltpu.CompilerParams(
            collective_id=0, has_side_effects=True, vmem_limit_bytes=56 * 1024 * 1024
        ),
    )(*operands)


def solution(mesh):
    rows = P(("section", "rep"), None, "tp")
    slots = P(None, ("section", "rep"), "tp")
    whole = P(None, ("section", "rep"), None)
    return jax.shard_map(
        on_device,
        mesh=mesh,
        in_specs=(
            rows,
            rows,
            rows,
            rows,
            P(),
            P(),
            rows,
            rows,
            P("tp", None),
            P(),
            whole,
            slots,
            slots,
            slots,
            slots,
            slots,
            slots,
            slots,
        ),
        out_specs=(rows, whole, slots),
        check_vma=False,
    )
```

time: 299 us -> 54.4 us (0.18)
  waiting for transfers between devices: 158 us -> 0 us
  Pallas kernels: 0 us -> 49.1 us
  starting transfers between devices: 40.6 us -> 0 us
  matrix products: 35.3 us -> 0 us
  local copies, waits for them, and re-layouts: 28 us -> 4.48 us
  other arithmetic: 20.6 us -> 0 us
  between operations: 14.7 us -> 0.66 us
    all_to_all x6 -> x0, waiting for transfers between devices: 93 us -> none  [the longest x1 40.2 us: section_leg(): lax.all_to_all(blocked(states, count), 'section', split_axis=0, concat_ax...]
    psum x1 -> x0, waiting for transfers between devices: 64.8 us -> none  [on_device(): summed = lax.psum(projected, 'tp')]
    pallas_call x0 -> x1, Pallas kernels: none -> 49.1 us  [on_device(): pl.pallas_call(functools.partial(body, dims), out_shape=(jax.ShapeDtypeSt...]
    all_to_all x6 -> x0, starting transfers between devices: 40.4 us -> none  [the longest x1 11.5 us: rep_leg(): lax.all_to_all(blocked(keys_part, count), 'rep', split_axis=0, concat_axi...]
    dot_general x23 -> x0, matrix products: 35.3 us -> none  [the longest x4 12.2 us: on_device(): linear = jnp.einsum('rhd,rhde->rhe', query_now, carried, precision=HIGHEST)]
    gather x10 -> x0, local copies, waits for them, and re-layouts: 19.2 us -> none  [the longest x9 18.5 us: reorder(): return tuple((jnp.take(piece, index, axis=0) for piece in parts))]
    reshape x4 -> x0, other arithmetic: 6.45 us -> none  [the longest x2 4.41 us: blocked(): return piece.reshape((count, -1) + piece.shape[1:])]
    select_n x8 -> x0, other arithmetic: 4.49 us -> none  [the longest x5 4.39 us: reorder(): return tuple((jnp.take(piece, index, axis=0) for piece in parts))]
  transfers between devices with their start and end apart: 7 -> 0, of which waited for: 6 -> 0; matrix products, arithmetic and copies ran while one was open for 17% -> 0% of each run, Pallas kernels for 0% -> 0%
where the time goes in v1:
time: 54.4 us; the launch traced here: 54.3 us
  Pallas kernels  49.1 us (90%)
  local copies, waits for them, and re-layouts  4.48 us (8%)
  between operations  0.66 us (1%)
    pallas_call x1, Pallas kernels, on_device(): pl.pallas_call(functools.partial(body, dims), out_shape=(jax.ShapeDtypeSt...  49.1 us
    unnamed x7, local copies, waits for them, and re-layouts  4.48 us

profile of v1, /device:TPU:1, one launch (start us, length us, event | category | flops | bytes accessed | tf_op | source)
XLA Modules:
  0.0 54.3 jit_solution(17596608128495974862)
XLA Ops:
  0.6 49.1 %shard_map.193 = (bf16[8,256,512]{2,1,0:T(8,128)(2,1)}, bf16[4,8,6144]{2,1,0:T(8,128)(2,1)}, bf16[4,8,1024]{2,1,0:T(8,128)(2,1)}) custom-call(bf16[8,256,512]{2,1,0:T(8,128)(2,1)} %pq_hbm.1, bf16[8,256,512]{2,1,0:T(8,128)(2,1)} %pk_hbm.1, bf16[8,256,512]{2,1,0:T(8,128)(2,1)} %pv_hbm.1, f32[8,4,256]{2,1,0:T(4,128)} %bitcast.4, s32[256]{0:T(256)} %len_hbm.1, ...), custom_call_target="tpu_custom_call" | custom-call | tf_op jit(solution)/shard_map/pallas_call | solution.py:635
  49.8 0.0 copy-start
  49.8 0.0 copy-start.1
  49.8 3.1 %copy.24 = bf16[8,256,512]{2,1,0:T(8,128)(2,1)} copy(bf16[8,256,512]{2,1,0:T(8,128)(2,1)} %get-tuple-element.6) | data formatting | bytes 4194304
  52.9 0.0 copy-done
  52.9 0.7 %copy.25 = bf16[4,8,6144]{2,1,0:T(8,128)(2,1)} copy(bf16[4,8,6144]{2,1,0:T(8,128)(2,1)S(1)} %copy-done) | data formatting | bytes 786432
  53.6 0.0 copy-done.1
  53.6 0.6 %copy.26 = bf16[4,8,1024]{2,1,0:T(8,128)(2,1)} copy(bf16[4,8,1024]{2,1,0:T(8,128)(2,1)S(1)} %copy-done.1) | data formatting | bytes 131072
Async XLA Ops:
  49.8 3.1 %copy-start = (bf16[4,8,6144]{2,1,0:T(8,128)(2,1)S(1)}, bf16[4,8,6144]{2,1,0:T(8,128)(2,1)}, u32[]{:S(2)}) copy-start(bf16[4,8,6144]{2,1,0:T(8,128)(2,1)} %get-tuple-element.7) | copy-start | bytes 1179652
  49.8 3.9 %copy-start.1 = (bf16[4,8,1024]{2,1,0:T(8,128)(2,1)S(1)}, bf16[4,8,1024]{2,1,0:T(8,128)(2,1)}, u32[]{:S(2)}) copy-start(bf16[4,8,1024]{2,1,0:T(8,128)(2,1)} %get-tuple-element.8) | copy-start | bytes 196612

commit v2 on v1

--- a/solution.py
+++ b/solution.py
@@ -59,9 +59,9 @@
     fq_hbm,
     fk_hbm,
     fv_hbm,
-    po_hbm,
-    do_hbm,
-    so_hbm,
+    po,
+    do,
+    so,
     pq,
     pk,
     pv,
@@ -81,11 +81,10 @@
     fq,
     fk,
     fv,
-    po,
-    so,
     rowf,
-    decf,
     colm,
+    colw,
+    state,
     own,
     gamma,
     sel_lin,
@@ -96,7 +95,9 @@
     send_r,
     recv_r,
     send_s,
-    recv_s,
+    recv_a,
+    send_b,
+    recv_b,
     res_s,
     send_t,
     recv_t,
@@ -105,18 +106,19 @@
     recv_p,
     ss_send,
     ss_recv,
-    ag,
     in_sem,
-    out_sem,
     q_sem,
     r_sem,
-    s_sem,
+    a_sem,
+    b_sem,
     t_sem,
     rs_send,
     rs_recv,
-    sib_sem,
+    ss_sem,
     ag_send,
     ag_recv,
+    pass_send,
+    pass_recv,
 ):
     sections, reps, tps, held, length, heads, steps, q_heads, model = dims
     groups = sections * reps
@@ -133,27 +135,42 @@
     lin_rows = heads * steps
     soft_rows = q_heads * steps
 
+    owners = tps // 2
+    sibling = (me_s, me_r, me_p + 1 - 2 * me_c)
+
+    deep = 2 * sections
+    across = reps // 2
+    me_z = (me_r // across) * sections + me_s
+    me_x = lax.rem(me_r, across)
+
+    def ring_step(n, size):
+        return size // 2 + ((n + 1) // 2) * (1 - 2 * lax.rem(n, 2)) + size
+
+    def far_first(m):
+        z = lax.rem(me_z + ring_step(m // across, deep), deep)
+        x = lax.rem(me_x + ring_step(lax.rem(m, across), across), across)
+        return lax.rem(z, sections), (z // sections) * across + x
+
+    def along_y(off):
+        return lax.rem(me_y + off, owners)
+
     barrier = pltpu.get_barrier_semaphore()
 
-    def greet(off, carry):
-        peer = lax.rem(me_g + off, groups)
+    def greet(m, carry):
+        peer_s, peer_r = far_first(m)
         pl.semaphore_signal(
-            barrier, inc=1, device_id=(peer // reps, lax.rem(peer, reps), me_p), device_id_type=MESH
+            barrier, inc=1, device_id=(peer_s, peer_r, me_p), device_id_type=MESH
         )
         return carry
 
-    lax.fori_loop(1, groups, greet, 0)
-
-    def greet_tp(off, carry):
+    lax.fori_loop(0, groups - 1, greet, 0)
+    for off in range(1, tps):
         pl.semaphore_signal(
             barrier,
             inc=1,
             device_id=(me_s, me_r, lax.rem(me_p + off, tps)),
             device_id_type=MESH,
         )
-        return carry
-
-    lax.fori_loop(1, tps, greet_tp, 0)
 
     y0 = me_y * per_owner
     col0 = pl.multiple_of(me_c * half, LANES)
@@ -216,30 +233,63 @@
     blocks = dot(spread_lin, by_row(sq, heads)).astype(BF16)
     send_q[...] = blocks.reshape(reps, lin_rows, LANES)
 
+    for name in ("fq", "fk", "fv"):
+        loads[name].wait()
+    soft_blocks = dot(spread(soft_rows, slot_of), by_row(fq, q_heads)).astype(BF16)
+    send_s[:, :soft_rows, :] = soft_blocks.reshape(reps, soft_rows, LANES)
+    fresh = jnp.concatenate([by_row(fk, 1).astype(F32), by_row(fv, 1).astype(F32)], axis=0)
+    fresh_spread = spread_lin[:, : 2 * steps * held]
+    fresh_blocks = dot(fresh_spread, fresh.astype(BF16)).astype(BF16)
+    send_s[:, soft_rows:, :] = fresh_blocks.reshape(reps, lin_rows, LANES)
+
     pl.semaphore_wait(barrier, groups - 1 + tps - 1)
 
     def to_groups(src, dst, sems):
-        def one(off, carry):
-            peer = lax.rem(me_g + off, groups)
-            peer_r = lax.rem(peer, reps)
+        def one(m, carry):
+            peer_s, peer_r = far_first(m)
             pltpu.make_async_remote_copy(
                 src_ref=src.at[peer_r],
                 dst_ref=dst.at[me_g],
                 send_sem=sems.at[0],
                 recv_sem=sems.at[1],
-                device_id=(peer // reps, peer_r, me_p),
+                device_id=(peer_s, peer_r, me_p),
                 device_id_type=MESH,
             ).start()
             return carry
 
-        lax.fori_loop(1, groups, one, 0)
+        lax.fori_loop(0, groups - 1, one, 0)
         dst[me_g] = src[me_r]
 
     def all_bytes(dst, sem):
-        view = dst.at[pl.ds(0, groups - 1)]
+        view = dst.at[pl.ds(0, dst.shape[0] - 1)]
         pltpu.make_async_copy(view, view, sem).wait()
 
+    def rep_copy(off):
+        peer_r = lax.rem(me_r + off, reps)
+        return pltpu.make_async_remote_copy(
+            src_ref=send_s.at[peer_r],
+            dst_ref=recv_a.at[me_r],
+            send_sem=a_sem.at[0],
+            recv_sem=a_sem.at[1],
+            device_id=(me_s, peer_r, me_p),
+            device_id_type=MESH,
+        )
+
+    def section_copy(off):
+        peer_s = lax.rem(me_s + off, sections)
+        return pltpu.make_async_remote_copy(
+            src_ref=send_b.at[peer_s],
+            dst_ref=recv_b.at[me_s],
+            send_sem=b_sem.at[0],
+            recv_sem=b_sem.at[1],
+            device_id=(peer_s, me_r, me_p),
+            device_id_type=MESH,
+        )
+
     to_groups(send_q, recv_q, q_sem)
+    for off in range(1, reps):
+        rep_copy(off).start()
+    recv_a[me_r] = send_s[me_r]
 
     loads["dg"].wait()
     loads["len"].wait()
@@ -260,20 +310,39 @@
     upto_t = one_hot(iota((length, length), 1) <= iota((length, length), 0))
     cum_rows = (dot(p1, upto) + dot(p2, upto) + dot(p3, upto)) * LOG2E
     cum_cols = (dot_nt(upto_t, p1) + dot_nt(upto_t, p2) + dot_nt(upto_t, p3)) * LOG2E
-    decays = jnp.where(inside, jnp.exp2(cum_rows[:, length - 1 :] - cum_rows), 0.0)
     shape = (length, count)
     len_cols = jnp.zeros(shape, jnp.int32)
     for k in range(held):
         len_cols = jnp.where(iota(shape, 1) // heads == k, own_len[k], len_cols)
-    cum_cols = jnp.where(iota(shape, 0) < len_cols, cum_cols, -jnp.inf)
+    inside_cols = iota(shape, 0) < len_cols
+    decays = jnp.where(inside_cols, jnp.exp2(cum_cols[length - 1 :] - cum_cols), 0.0)
+    cum_cols = jnp.where(inside_cols, cum_cols, -jnp.inf)
     for k in range(held):
         rows = slice(k * heads, (k + 1) * heads)
         rowf[k] = cum_rows[rows]
-        decf[k] = decays[rows]
         colm[k] = cum_cols[:, rows]
+        colw[k] = decays[:, rows]
 
     loads["pk"].wait()
     loads["pv"].wait()
+
+    def remember(k, carry):
+        for h in range(heads):
+            lanes = slice(h * LANES, (h + 1) * LANES)
+            high, low = split_two(pv[k, :, lanes].astype(F32) * colw[k, :, h : h + 1])
+            both = lax.dot_general(
+                pk[k, :, lanes],
+                jnp.concatenate([high, low], axis=1),
+                (((0,), (0,)), ((), ())),
+                preferred_element_type=F32,
+            )
+            high, low = split_two(both[:, :LANES] + both[:, LANES:])
+            state[k, h, :LANES, :] = high
+            state[k, h, LANES:, :] = low
+        return carry
+
+    lax.fori_loop(0, held, remember, 0)
+
     loads["pq"].wait()
     mid = length // 2
 
@@ -293,44 +362,10 @@
             low = jnp.concatenate([low_left, low_right], axis=1)
             po[k, :mid, lanes] = dot(top, values[:mid]).astype(BF16)
             po[k, mid:, lanes] = dot(low, values).astype(BF16)
-        pltpu.make_async_copy(po.at[k], po_hbm.at[k], out_sem.at[k]).start()
         return carry
 
-    marks = [0, held // 4, held // 2 + 1, held // 2 + 2, held]
-    lax.fori_loop(marks[0], marks[1], prompt, 0)
-
-    for name in ("fq", "fk", "fv", "sk", "sv", "sg"):
+    for name in ("sk", "sv", "sg"):
         loads[name].wait()
-    soft_blocks = dot(spread(soft_rows, slot_of), by_row(fq, q_heads)).astype(BF16)
-    send_s[:, :soft_rows, :] = soft_blocks.reshape(reps, soft_rows, LANES)
-    fresh = jnp.concatenate([by_row(fk, 1).astype(F32), by_row(fv, 1).astype(F32)], axis=0)
-    fresh_spread = spread_lin[:, : 2 * steps * held]
-    fresh_blocks = dot(fresh_spread, fresh.astype(BF16)).astype(BF16)
-    send_s[:, soft_rows:, :] = fresh_blocks.reshape(reps, lin_rows, LANES)
-
-    target_rep = [lax.rem(dg_s[first + k], reps) for k in range(held)]
-    bound_for = []
-    for r in range(reps):
-        found = jnp.int32(0)
-        for k in range(held):
-            found = jnp.where(target_rep[k] == r, k, found)
-        bound_for.append(found)
-    all_bytes(recv_q, q_sem.at[1])
-    head_of_row = iota((lin_rows, length), 0) // steps
-    for k in range(held):
-        asked = recv_q[dg_s[first + k]]
-        result = jnp.zeros((2 * lin_rows, LANES), F32)
-        for h in range(heads):
-            lanes = slice(h * LANES, (h + 1) * LANES)
-            weights = dot_nt(asked, pk[k, :, lanes]) * decf[k, h : h + 1, :]
-            high, low = split_two(jnp.where(head_of_row == h, weights, 0.0))
-            result = result + dot(jnp.concatenate([high, low], axis=0), pv[k, :, lanes])
-        res_q[k] = (result[:lin_rows] + result[lin_rows:]).astype(BF16)
-    for r in range(reps):
-        send_r[r] = res_q[bound_for[r]]
-    to_groups(send_r, recv_r, r_sem)
-    to_groups(send_s, recv_s, s_sem)
-
     eye = jnp.where(iota((held, held), 0) == iota((held, held), 1), 1.0, 0.0)
     gates = [dot_nt(eye, sg[i], lax.Precision.HIGHEST) for i in range(steps)]
     for h in range(heads):
@@ -356,56 +391,107 @@
         return jnp.where(same, picked, 0.0).astype(BF16)
 
     sel_lin[...] = pick(lin_rows, slot_lin)
-    lax.fori_loop(marks[1], marks[2], prompt, 0)
+    target_rep = [lax.rem(dg_s[first + k], reps) for k in range(held)]
+    bound_for = []
+    for r in range(reps):
+        found = jnp.int32(0)
+        for k in range(held):
+            found = jnp.where(target_rep[k] == r, k, found)
+        bound_for.append(found)
+    each = held // sections
+    onward = []
+    for s in range(sections):
+        chosen = [jnp.int32(0)] * each
+        seen = jnp.int32(0)
+        for k in range(held):
+            group = dg_s[(s * reps + me_r) * held + k]
+            hit = lax.div(group, reps) == me_s
+            for c in range(each):
+                chosen[c] = jnp.where(hit & (seen == c), lax.rem(group, reps), chosen[c])
+            seen = seen + jnp.where(hit, 1, 0)
+        onward.append(chosen)
+    all_bytes(recv_q, q_sem.at[1])
+    head_of_row = iota((lin_rows, LANES), 0) // steps
+    for k in range(held):
+        asked = recv_q[dg_s[first + k]].astype(F32)
+        apart = []
+        for h in range(heads):
+            apart += [jnp.where(head_of_row == h, asked, 0.0).astype(BF16)] * 2
+        states = state[k].reshape(2 * heads * LANES, LANES)
+        res_q[k] = dot(jnp.concatenate(apart, axis=1), states).astype(BF16)
+    for r in range(reps):
+        send_r[r] = res_q[bound_for[r]]
+    to_groups(send_r, recv_r, r_sem)
+
+    all_bytes(recv_a, a_sem.at[1])
+    for s in range(sections):
+        for c in range(each):
+            send_b[s, c] = recv_a[onward[s][c]]
+    for off in range(1, sections):
+        section_copy(off).start()
+    recv_b[me_s] = send_b[me_s]
+
+    sel_soft[...] = pick(soft_rows, slot_of)
+    early = held // 2
+    lax.fori_loop(0, early, prompt, 0)
 
     loads["w"].wait()
     all_bytes(recv_r, r_sem.at[1])
     carried = dot(sel_lin[...], recv_r[...].reshape(groups * lin_rows, LANES))
     hidden = []
     for i in range(steps):
-        across = []
+        over_heads = []
         for h in range(heads):
             lanes = slice(h * LANES, (h + 1) * LANES)
             rows = slice((h * steps + i) * held, (h * steps + i + 1) * held)
-            across.append(gamma[i, :, lanes] * carried[rows] + own[i, :, lanes])
-        hidden.append(jnp.concatenate(across, axis=1))
+            over_heads.append(gamma[i, :, lanes] * carried[rows] + own[i, :, lanes])
+        hidden.append(jnp.concatenate(over_heads, axis=1))
     hidden = jnp.concatenate(hidden, axis=0).astype(BF16)
-    pieces = 4
-    wide = model // pieces
-    owners = tps // 2
-
-    def piece_copy(c, owner, source):
+    wide = half // 2
+    other0 = pl.multiple_of((1 - me_c) * half, LANES)
+
+    by_distance = sorted(range(1, owners), key=lambda o: -min(o, owners - o))
+
+    def sum_copy(which, q, off):
+        owner = along_y(off)
+        core = me_c if which else 1 - me_c
         return pltpu.make_async_remote_copy(
-            src_ref=part_b.at[pl.ds(owner * per_owner, per_owner), :, c * wide : (c + 1) * wide],
-            dst_ref=recv_p.at[source, c % 2],
-            send_sem=rs_send.at[owner, c],
-            recv_sem=rs_recv.at[source, c % 2],
-            device_id=(me_s, me_r, owner * 2 + c // 2),
+            src_ref=part_b.at[which, q, pl.ds(owner * per_owner, per_owner)],
+            dst_ref=recv_p.at[me_p, q],
+            send_sem=rs_send.at[owner, which, q],
+            recv_sem=rs_recv.at[me_p, q],
+            device_id=(me_s, me_r, owner * 2 + core),
             device_id_type=MESH,
         )
 
-    for c in range(pieces):
-        cols = slice(c * wide, (c + 1) * wide)
-        partial = dot(hidden, w[:, cols])
-        for i in range(steps):
-            rows = partial[i * held : (i + 1) * held]
-            part_f[i, :, cols] = rows
-            part_b[i, :, cols] = rows.astype(BF16)
-
-        for off in range(owners):
-            owner = lax.rem(me_y + 1 + off, owners)
-
-            @pl.when((owner != me_y) | (me_c != c // 2))
-            def _():
-                piece_copy(c, owner, me_p).start()
+    def sum_copies(which):
+        return by_distance if which else by_distance + [0]
+
+    for which in range(2):
+        start = col0 if which else other0
+        for q in range(2):
+            cols = pl.ds(pl.multiple_of(start + q * wide, LANES), wide)
+            partial = dot(hidden, w[:, cols])
+            for i in range(steps):
+                rows = partial[i * held : (i + 1) * held]
+                part_b[which, q, i] = rows.astype(BF16)
+                if which:
+                    part_f[q, i] = rows
+            for off in sum_copies(which):
+                sum_copy(which, q, off).start()
 
     loads["ck"].wait()
     loads["cv"].wait()
-    all_bytes(recv_s, s_sem.at[1])
+    all_bytes(recv_b, b_sem.at[1])
     scale = LOG2E / math.sqrt(LANES)
 
     def soft(k, carry):
-        block = recv_s[dg_s[first + k]]
+        section = lax.div(dg_s[first + k], reps)
+        place_of = jnp.int32(0)
+        for k2 in range(held):
+            same = (lax.div(dg_s[first + k2], reps) == section) & (k2 < k)
+            place_of = place_of + jnp.where(same, 1, 0)
+        block = recv_b[section, jnp.minimum(place_of, each - 1)]
         asked = block[:soft_rows]
         fresh_rows = block[soft_rows:]
         scores = dot_nt(asked, ck[k]) * scale
@@ -433,17 +519,16 @@
     for r in range(reps):
         send_t[r] = res_s[bound_for[r]]
     to_groups(send_t, recv_t, t_sem)
-    sel_soft[...] = pick(soft_rows, slot_of)
-
     loads["si"].wait()
     loads["gain"].wait()
     summed = []
     for part in range(2):
-        cols = pl.ds(pl.multiple_of(me_c * half + part * wide, LANES), wide)
         here = slice(part * wide, (part + 1) * wide)
-        value = part_f[pl.ds(y0, per_owner), :, cols] + si[:, :, here].astype(F32)
-        for off in range(1, tps):
-            source = lax.rem(me_p + off, tps)
+        value = part_f[part, pl.ds(y0, per_owner)] + si[:, :, here].astype(F32)
+        sources = [me_p + 1 - 2 * me_c]
+        for off in reversed(by_distance):
+            sources += [along_y(off) * 2, along_y(off) * 2 + 1]
+        for source in sources:
             pltpu.make_async_copy(
                 recv_p.at[source, part], recv_p.at[source, part], rs_recv.at[source, part]
             ).wait()
@@ -452,40 +537,53 @@
     square = jnp.sum(summed[0] * summed[0], axis=2, keepdims=True)
     square = square + jnp.sum(summed[1] * summed[1], axis=2, keepdims=True)
     ss_send[...] = jnp.broadcast_to(square, ss_send.shape)
-    sibling = pltpu.make_async_remote_copy(
+    squares = pltpu.make_async_remote_copy(
         src_ref=ss_send,
         dst_ref=ss_recv,
-        send_sem=sib_sem.at[0],
-        recv_sem=sib_sem.at[1],
-        device_id=(me_s, me_r, me_p + 1 - 2 * me_c),
+        send_sem=ss_sem.at[0],
+        recv_sem=ss_sem.at[1],
+        device_id=sibling,
         device_id_type=MESH,
     )
-    sibling.start()
-    sibling.wait()
+    squares.start()
+    squares.wait()
     mean = (square + ss_recv[:, :, 0:1]) / model
     spread_of = jnp.sqrt(mean + 1e-06)
     for part in range(2):
         here = slice(part * wide, (part + 1) * wide)
+        cols = pl.ds(pl.multiple_of(col0 + part * wide, LANES), wide)
         gains = gain[:, here].reshape(1, 1, wide)
-        ag[:, :, here] = (summed[part] / spread_of * gains).astype(BF16)
-    place = do_hbm.at[pl.ds(y0, per_owner), :, pl.ds(col0, half)]
-    mine_out = pltpu.make_async_copy(ag, place, out_sem.at[held])
-    mine_out.start()
-
-    def gather_copy(peer):
+        do[pl.ds(y0, per_owner), :, cols] = (summed[part] / spread_of * gains).astype(BF16)
+
+    def place(y):
+        return do.at[pl.ds(y * per_owner, per_owner), :, pl.ds(col0, half)]
+
+    def gather_copy(off):
+        peer = along_y(off)
         return pltpu.make_async_remote_copy(
-            src_ref=ag,
-            dst_ref=place,
+            src_ref=place(me_y),
+            dst_ref=place(me_y),
             send_sem=ag_send.at[peer],
-            recv_sem=ag_recv.at[me_p],
-            device_id=(me_s, me_r, peer),
+            recv_sem=ag_recv.at[me_y],
+            device_id=(me_s, me_r, peer * 2 + me_c),
             device_id_type=MESH,
         )
 
-    for off in range(1, tps):
-        gather_copy(lax.rem(me_p + off, tps)).start()
-
-    lax.fori_loop(marks[2], marks[4], prompt, 0)
+    def pass_copy(y):
+        return pltpu.make_async_remote_copy(
+            src_ref=place(y),
+            dst_ref=place(y),
+            send_sem=pass_send.at[y],
+            recv_sem=pass_recv.at[y],
+            device_id=sibling,
+            device_id_type=MESH,
+        )
+
+    for off in by_distance:
+        gather_copy(off).start()
+    pass_copy(me_y).start()
+
+    lax.fori_loop(early, held, prompt, 0)
 
     all_bytes(recv_t, t_sem.at[1])
     placed = dot(sel_soft[...], recv_t[...].reshape(groups * soft_rows, LANES))
@@ -493,29 +591,36 @@
         for i in range(steps):
             rows = slice((a * steps + i) * held, (a * steps + i + 1) * held)
             so[i, :, a * LANES : (a + 1) * LANES] = placed[rows].astype(BF16)
-    soft_out = pltpu.make_async_copy(so, so_hbm, out_sem.at[held + 1])
-    soft_out.start()
+
+    for off in reversed(by_distance):
+        source = along_y(off)
+        pltpu.make_async_copy(place(source), place(source), ag_recv.at[source]).wait()
+        pass_copy(source).start()
 
     all_bytes(recv_q, q_sem.at[0])
     all_bytes(recv_r, r_sem.at[0])
-    all_bytes(recv_s, s_sem.at[0])
+    all_bytes(recv_a, a_sem.at[0])
+    all_bytes(recv_b, b_sem.at[0])
     all_bytes(recv_t, t_sem.at[0])
-    for c in range(pieces):
-        for off in range(owners):
-            owner = lax.rem(me_y + 1 + off, owners)
-
-            @pl.when((owner != me_y) | (me_c != c // 2))
-            def _():
-                piece_copy(c, owner, me_p).wait_send()
-
-    for k in range(held):
-        pltpu.make_async_copy(po.at[k], po_hbm.at[k], out_sem.at[k]).wait()
-    soft_out.wait()
-    mine_out.wait()
-    for off in range(1, tps):
-        peer = lax.rem(me_p + off, tps)
-        gather_copy(peer).wait_send()
-        pltpu.make_async_copy(ag, ag, ag_recv.at[peer]).wait()
+    for which in range(2):
+        for q in range(2):
+            for off in sum_copies(which):
+                sum_copy(which, q, off).wait_send()
+    for off in range(1, owners):
+        gather_copy(off).wait_send()
+    for y in range(owners):
+        pass_copy(y).wait()
+
+
+def write_out(po, do, so, po_hbm, do_hbm, so_hbm, sem):
+    held = po.shape[0]
+    copies = [pltpu.make_async_copy(po.at[k], po_hbm.at[k], sem.at[k]) for k in range(held)]
+    copies.append(pltpu.make_async_copy(do, do_hbm, sem.at[held]))
+    copies.append(pltpu.make_async_copy(so, so_hbm, sem.at[held + 1]))
+    for copy in copies:
+        copy.start()
+    for copy in copies:
+        copy.wait()
 
 
 def on_device(
@@ -594,11 +699,10 @@
         vmem((steps, held, q_heads * LANES), BF16),
         vmem((steps, held, LANES), BF16),
         vmem((steps, held, LANES), BF16),
-        vmem((held, length, width), BF16),
-        vmem((steps, held, q_heads * LANES), BF16),
-        vmem((held, heads, length), F32),
         vmem((held, heads, length), F32),
         vmem((held, length, heads), F32),
+        vmem((held, length, heads), F32),
+        vmem((held, heads, 2 * LANES, LANES), BF16),
         vmem((steps, held, width), F32),
         vmem((steps, held, width), F32),
         vmem((lin_rows * held, lin_rows * groups), BF16),
@@ -609,43 +713,54 @@
         vmem((reps, lin_rows, LANES), BF16),
         vmem((groups, lin_rows, LANES), BF16),
         vmem((reps, soft_rows + lin_rows, LANES), BF16),
-        vmem((groups, soft_rows + lin_rows, LANES), BF16),
+        vmem((reps, soft_rows + lin_rows, LANES), BF16),
+        vmem((sections, held // sections, soft_rows + lin_rows, LANES), BF16),
+        vmem((sections, held // sections, soft_rows + lin_rows, LANES), BF16),
         vmem((held, soft_rows, LANES), BF16),
         vmem((reps, soft_rows, LANES), BF16),
         vmem((groups, soft_rows, LANES), BF16),
-        vmem((steps, held, model), F32),
-        vmem((steps, held, model), BF16),
+        vmem((2, steps, held, half // 2), F32),
+        vmem((2, 2, steps, held, half // 2), BF16),
         vmem((tps, 2, per_owner, held, half // 2), BF16),
         vmem((per_owner, held, LANES), F32),
         vmem((per_owner, held, LANES), F32),
-        vmem((per_owner, held, half), BF16),
         dma((19,)),
-        dma((held + 2,)),
         dma((2,)),
         dma((2,)),
         dma((2,)),
         dma((2,)),
-        dma((tps // 2, 4)),
+        dma((2,)),
+        dma((tps // 2, 2, 2)),
         dma((tps, 2)),
         dma((2,)),
-        dma((tps,)),
-        dma((tps,)),
+        dma((tps // 2,)),
+        dma((tps // 2,)),
+        dma((tps // 2,)),
+        dma((tps // 2,)),
     ]
     anywhere = pl.BlockSpec(memory_space=pl.ANY)
-    return pl.pallas_call(
+    results = pl.pallas_call(
         functools.partial(body, dims),
         out_shape=(
-            jax.ShapeDtypeStruct((held, length, width), BF16),
-            jax.ShapeDtypeStruct((steps, held, model), BF16),
-            jax.ShapeDtypeStruct((steps, held, q_heads * LANES), BF16),
+            vmem((held, length, width), BF16),
+            vmem((steps, held, model), BF16),
+            vmem((steps, held, q_heads * LANES), BF16),
         ),
         in_specs=[anywhere] * len(operands),
-        out_specs=(anywhere,) * 3,
+        out_specs=(pl.BlockSpec(memory_space=vmem),) * 3,
         scratch_shapes=scratch,
         compiler_params=pltpu.CompilerParams(
             collective_id=0, has_side_effects=True, vmem_limit_bytes=56 * 1024 * 1024
         ),
     )(*operands)
+    results = [pltpu.with_memory_space_constraint(x, pltpu.VMEM) for x in results]
+    return pl.pallas_call(
+        write_out,
+        out_shape=[jax.ShapeDtypeStruct(array.shape, array.dtype) for array in results],
+        in_specs=[anywhere] * 3,
+        out_specs=[anywhere] * 3,
+        scratch_shapes=[dma((held + 2,))],
+    )(*results)
 
 
 def solution(mesh):

time: 54.4 us -> 43.4 us (0.80)
  Pallas kernels: 49.1 us -> 42.6 us
  local copies, waits for them, and re-layouts: 4.48 us -> 0 us
    pallas_call x1 -> x2, Pallas kernels: 49.1 us -> 42.6 us  [the longest x1 41.1 us: on_device(): pl.pallas_call(functools.partial(body, dims), out_shape=(vmem((held, leng...]
    unnamed x7 -> x0, local copies, waits for them, and re-layouts: 4.48 us -> none
where the time goes in v2:
time: 43.4 us; the launch traced here: 43.3 us
  Pallas kernels  42.6 us (98%)
  between operations  0.65 us (1%)
    pallas_call x1, Pallas kernels, on_device(): pl.pallas_call(functools.partial(body, dims), out_shape=(vmem((held, leng...  41.1 us
    pallas_call x1, Pallas kernels, on_device(): pl.pallas_call(write_out, out_shape=[jax.ShapeDtypeStruct(array.shape, ar...  1.54 us

profile of v2, /device:TPU:1, one launch (start us, length us, event | category | flops | bytes accessed | tf_op | source)
XLA Modules:
  0.0 43.3 jit_solution(9528027329313361590)
XLA Ops:
  0.6 41.1 %shard_map.193 = (bf16[8,256,512]{2,1,0:T(8,128)(2,1)S(1)}, bf16[4,8,6144]{2,1,0:T(8,128)(2,1)S(1)}, bf16[4,8,1024]{2,1,0:T(8,128)(2,1)S(1)}) custom-call(bf16[8,256,512]{2,1,0:T(8,128)(2,1)} %pq_hbm.1, bf16[8,256,512]{2,1,0:T(8,128)(2,1)} %pk_hbm.1, bf16[8,256,512]{2,1,0:T(8,128)(2,1)} %pv_hbm.1, f32[8,4,256]{2,1,0:T(4,128)} %bitcast.4, s32[256]{0:T(256)} %len_hbm.1, ...), custom_call_target="tpu_custom_call" | custom-call | tf_op jit(solution)/shard_map/pallas_call | solution.py:742
  41.7 1.5 %shard_map.194 = (bf16[8,256,512]{2,1,0:T(8,128)(2,1)}, bf16[4,8,6144]{2,1,0:T(8,128)(2,1)}, bf16[4,8,1024]{2,1,0:T(8,128)(2,1)}) custom-call(bf16[8,256,512]{2,1,0:T(8,128)(2,1)S(1)} %get-tuple-element.6.po, bf16[4,8,6144]{2,1,0:T(8,128)(2,1)S(1)} %get-tuple-element.7.do, bf16[4,8,1024]{2,1,0:T(8,128)(2,1)S(1)} %get-tuple-element.8.so), custom_call_target="tpu_custom_call" | custom-call | tf_op jit(solution)/shard_map/pallas_call | solution.py:757

commit v3 on v2

--- a/solution.py
+++ b/solution.py
@@ -143,27 +143,34 @@
     me_z = (me_r // across) * sections + me_s
     me_x = lax.rem(me_r, across)
 
-    def ring_step(n, size):
-        return size // 2 + ((n + 1) // 2) * (1 - 2 * lax.rem(n, 2)) + size
-
-    def far_first(m):
-        z = lax.rem(me_z + ring_step(m // across, deep), deep)
-        x = lax.rem(me_x + ring_step(lax.rem(m, across), across), across)
-        return lax.rem(z, sections), (z // sections) * across + x
+    def ring(me, size):
+        return {d: lax.rem(me + d, size) for d in range(size)}
+
+    def hops(d, size):
+        return min(d, size - d)
+
+    z_at = ring(me_z, deep)
+    x_at = ring(me_x, across)
+    section_at = {d: lax.rem(z, sections) for d, z in z_at.items()}
+    rep_at = {d: lax.div(z, sections) * across for d, z in z_at.items()}
+    far_first = sorted(
+        ((dz, dx) for dz in range(deep) for dx in range(across) if dz or dx),
+        key=lambda d: -hops(d[0], deep) - hops(d[1], across),
+    )
+    y_at = ring(me_y, owners)
 
     def along_y(off):
-        return lax.rem(me_y + off, owners)
+        return y_at[off]
 
     barrier = pltpu.get_barrier_semaphore()
 
-    def greet(m, carry):
-        peer_s, peer_r = far_first(m)
+    for dz, dx in far_first:
         pl.semaphore_signal(
-            barrier, inc=1, device_id=(peer_s, peer_r, me_p), device_id_type=MESH
+            barrier,
+            inc=1,
+            device_id=(section_at[dz], rep_at[dz] + x_at[dx], me_p),
+            device_id_type=MESH,
         )
-        return carry
-
-    lax.fori_loop(0, groups - 1, greet, 0)
     for off in range(1, tps):
         pl.semaphore_signal(
             barrier,
@@ -245,19 +252,16 @@
     pl.semaphore_wait(barrier, groups - 1 + tps - 1)
 
     def to_groups(src, dst, sems):
-        def one(m, carry):
-            peer_s, peer_r = far_first(m)
+        for dz, dx in far_first:
+            peer_r = rep_at[dz] + x_at[dx]
             pltpu.make_async_remote_copy(
                 src_ref=src.at[peer_r],
                 dst_ref=dst.at[me_g],
                 send_sem=sems.at[0],
                 recv_sem=sems.at[1],
-                device_id=(peer_s, peer_r, me_p),
+                device_id=(section_at[dz], peer_r, me_p),
                 device_id_type=MESH,
             ).start()
-            return carry
-
-        lax.fori_loop(0, groups - 1, one, 0)
         dst[me_g] = src[me_r]
 
     def all_bytes(dst, sem):
@@ -549,41 +553,48 @@
     squares.wait()
     mean = (square + ss_recv[:, :, 0:1]) / model
     spread_of = jnp.sqrt(mean + 1e-06)
-    for part in range(2):
-        here = slice(part * wide, (part + 1) * wide)
+    def place(y, part):
         cols = pl.ds(pl.multiple_of(col0 + part * wide, LANES), wide)
-        gains = gain[:, here].reshape(1, 1, wide)
-        do[pl.ds(y0, per_owner), :, cols] = (summed[part] / spread_of * gains).astype(BF16)
-
-    def place(y):
-        return do.at[pl.ds(y * per_owner, per_owner), :, pl.ds(col0, half)]
-
-    def gather_copy(off):
+        return do.at[pl.ds(y * per_owner, per_owner), :, cols]
+
+    def gather_copy(off, part):
         peer = along_y(off)
         return pltpu.make_async_remote_copy(
-            src_ref=place(me_y),
-            dst_ref=place(me_y),
-            send_sem=ag_send.at[peer],
-            recv_sem=ag_recv.at[me_y],
+            src_ref=place(me_y, part),
+            dst_ref=place(me_y, part),
+            send_sem=ag_send.at[peer, part],
+            recv_sem=ag_recv.at[me_y, part],
             device_id=(me_s, me_r, peer * 2 + me_c),
             device_id_type=MESH,
         )
 
-    def pass_copy(y):
+    def pass_copy(y, part):
         return pltpu.make_async_remote_copy(
-            src_ref=place(y),
-            dst_ref=place(y),
-            send_sem=pass_send.at[y],
-            recv_sem=pass_recv.at[y],
+            src_ref=place(y, part),
+            dst_ref=place(y, part),
+            send_sem=pass_send.at[y, part],
+            recv_sem=pass_recv.at[y, part],
             device_id=sibling,
             device_id_type=MESH,
         )
 
-    for off in by_distance:
-        gather_copy(off).start()
-    pass_copy(me_y).start()
+    for part in range(2):
+        here = slice(part * wide, (part + 1) * wide)
+        gains = gain[:, here].reshape(1, 1, wide)
+        place(me_y, part)[...] = (summed[part] / spread_of * gains).astype(BF16)
+        for off in by_distance:
+            gather_copy(off, part).start()
+    for part in range(2):
+        pass_copy(me_y, part).start()
 
     lax.fori_loop(early, held, prompt, 0)
+
+    for part in range(2):
+        for off in reversed(by_distance):
+            source = along_y(off)
+            landed = place(source, part)
+            pltpu.make_async_copy(landed, landed, ag_recv.at[source, part]).wait()
+            pass_copy(source, part).start()
 
     all_bytes(recv_t, t_sem.at[1])
     placed = dot(sel_soft[...], recv_t[...].reshape(groups * soft_rows, LANES))
@@ -591,11 +602,6 @@
         for i in range(steps):
             rows = slice((a * steps + i) * held, (a * steps + i + 1) * held)
             so[i, :, a * LANES : (a + 1) * LANES] = placed[rows].astype(BF16)
-
-    for off in reversed(by_distance):
-        source = along_y(off)
-        pltpu.make_async_copy(place(source), place(source), ag_recv.at[source]).wait()
-        pass_copy(source).start()
 
     all_bytes(recv_q, q_sem.at[0])
     all_bytes(recv_r, r_sem.at[0])
@@ -606,10 +612,11 @@
         for q in range(2):
             for off in sum_copies(which):
                 sum_copy(which, q, off).wait_send()
-    for off in range(1, owners):
-        gather_copy(off).wait_send()
-    for y in range(owners):
-        pass_copy(y).wait()
+    for part in range(2):
+        for off in range(1, owners):
+            gather_copy(off, part).wait_send()
+        for y in range(owners):
+            pass_copy(y, part).wait()
 
 
 def write_out(po, do, so, po_hbm, do_hbm, so_hbm, sem):
@@ -733,10 +740,10 @@
         dma((tps // 2, 2, 2)),
         dma((tps, 2)),
         dma((2,)),
-        dma((tps // 2,)),
-        dma((tps // 2,)),
-        dma((tps // 2,)),
-        dma((tps // 2,)),
+        dma((tps // 2, 2)),
+        dma((tps // 2, 2)),
+        dma((tps // 2, 2)),
+        dma((tps // 2, 2)),
     ]
     anywhere = pl.BlockSpec(memory_space=pl.ANY)
     results = pl.pallas_call(

time: 43.4 us -> 41 us (0.945)
  Pallas kernels: 42.6 us -> 40.2 us
    pallas_call x1, Pallas kernels: 41.1 us -> 38.7 us  [on_device(): pl.pallas_call(functools.partial(body, dims), out_shape=(vmem((held, leng...]
where the time goes in v3:
time: 41 us; the launch traced here: 40.9 us
  Pallas kernels  40.2 us (98%)
  between operations  0.65 us (2%)
    pallas_call x1, Pallas kernels, on_device(): pl.pallas_call(functools.partial(body, dims), out_shape=(vmem((held, leng...  38.7 us
    pallas_call x1, Pallas kernels, on_device(): pl.pallas_call(write_out, out_shape=[jax.ShapeDtypeStruct(array.shape, ar...  1.54 us

profile of v3, /device:TPU:1, one launch (start us, length us, event | category | flops | bytes accessed | tf_op | source)
XLA Modules:
  0.0 40.9 jit_solution(8417275100874099579)
XLA Ops:
  0.6 38.7 %shard_map.193 = (bf16[8,256,512]{2,1,0:T(8,128)(2,1)S(1)}, bf16[4,8,6144]{2,1,0:T(8,128)(2,1)S(1)}, bf16[4,8,1024]{2,1,0:T(8,128)(2,1)S(1)}) custom-call(bf16[8,256,512]{2,1,0:T(8,128)(2,1)} %pq_hbm.1, bf16[8,256,512]{2,1,0:T(8,128)(2,1)} %pk_hbm.1, bf16[8,256,512]{2,1,0:T(8,128)(2,1)} %pv_hbm.1, f32[8,4,256]{2,1,0:T(4,128)} %bitcast.4, s32[256]{0:T(256)} %len_hbm.1, ...), custom_call_target="tpu_custom_call" | custom-call | tf_op jit(solution)/shard_map/pallas_call | solution.py:749
  39.3 1.5 %shard_map.194 = (bf16[8,256,512]{2,1,0:T(8,128)(2,1)}, bf16[4,8,6144]{2,1,0:T(8,128)(2,1)}, bf16[4,8,1024]{2,1,0:T(8,128)(2,1)}) custom-call(bf16[8,256,512]{2,1,0:T(8,128)(2,1)S(1)} %get-tuple-element.6.po, bf16[4,8,6144]{2,1,0:T(8,128)(2,1)S(1)} %get-tuple-element.7.do, bf16[4,8,1024]{2,1,0:T(8,128)(2,1)S(1)} %get-tuple-element.8.so), custom_call_target="tpu_custom_call" | custom-call | tf_op jit(solution)/shard_map/pallas_call | solution.py:764

commit v4 on v3

--- a/solution.py
+++ b/solution.py
@@ -13,6 +13,8 @@
 BF16 = jnp.bfloat16
 LOG2E = 1.0 / math.log(2.0)
 LANES = 128
+TILE = 16
+PARTS = 2
 
 
 def iota(shape, axis):
@@ -98,14 +100,14 @@
     recv_a,
     send_b,
     recv_b,
-    res_s,
     send_t,
     recv_t,
     part_f,
     part_b,
     recv_p,
-    ss_send,
-    ss_recv,
+    base_of,
+    gain_of,
+    rows_of,
     in_sem,
     q_sem,
     r_sem,
@@ -114,11 +116,9 @@
     t_sem,
     rs_send,
     rs_recv,
-    ss_sem,
     ag_send,
     ag_recv,
     pass_send,
-    pass_recv,
 ):
     sections, reps, tps, held, length, heads, steps, q_heads, model = dims
     groups = sections * reps
@@ -128,7 +128,6 @@
     me_p = lax.axis_index("tp")
     me_g = me_s * reps + me_r
     first = me_g * held
-    half = model // 2
     per_owner = steps * 2 // tps
     me_y = me_p // 2
     me_c = me_p % 2
@@ -180,7 +179,6 @@
         )
 
     y0 = me_y * per_owner
-    col0 = pl.multiple_of(me_c * half, LANES)
     loads = {}
     for place, (name, src, dst) in enumerate(
         (
@@ -201,8 +199,8 @@
             ("w", w_hbm, w),
             ("ck", ck_hbm, ck),
             ("cv", cv_hbm, cv),
-            ("si", si_hbm.at[pl.ds(y0, per_owner), :, pl.ds(col0, half)], si),
-            ("gain", gain_hbm.at[:, pl.ds(col0, half)], gain),
+            ("si", si_hbm.at[pl.ds(y0, per_owner)], si),
+            ("gain", gain_hbm, gain),
         )
     ):
         loads[name] = pltpu.make_async_copy(src, dst, in_sem.at[place])
@@ -439,6 +437,28 @@
     early = held // 2
     lax.fori_loop(0, early, prompt, 0)
 
+    mine_each = held // 2
+    owned = per_owner * mine_each
+    blocks_of = TILE // owned
+    wide = model // blocks_of
+    narrow = wide // PARTS
+    loads["si"].wait()
+    loads["gain"].wait()
+    block_row = iota((TILE, wide), 0) // owned
+    shape = (TILE, per_owner * held)
+    row = lax.rem(iota(shape, 0), owned)
+    wanted = (row // mine_each) * held + me_c * mine_each + lax.rem(row, mine_each)
+    own_rows = one_hot(wanted == iota(shape, 1))
+    inputs = jnp.concatenate([si[n].astype(F32) for n in range(per_owner)], axis=0).astype(BF16)
+    base = jnp.zeros((TILE, wide), F32)
+    gains = jnp.zeros((TILE, wide), F32)
+    for b in range(blocks_of):
+        cols = slice(b * wide, (b + 1) * wide)
+        base = jnp.where(block_row == b, dot(own_rows, inputs[:, cols]), base)
+        gains = jnp.where(block_row == b, gain[:, cols], gains)
+    base_of[...] = base
+    gain_of[...] = gains
+
     loads["w"].wait()
     all_bytes(recv_r, r_sem.at[1])
     carried = dot(sel_lin[...], recv_r[...].reshape(groups * lin_rows, LANES))
@@ -451,45 +471,41 @@
             over_heads.append(gamma[i, :, lanes] * carried[rows] + own[i, :, lanes])
         hidden.append(jnp.concatenate(over_heads, axis=1))
     hidden = jnp.concatenate(hidden, axis=0).astype(BF16)
-    wide = half // 2
-    other0 = pl.multiple_of((1 - me_c) * half, LANES)
-
     by_distance = sorted(range(1, owners), key=lambda o: -min(o, owners - o))
-
-    def sum_copy(which, q, off):
-        owner = along_y(off)
-        core = me_c if which else 1 - me_c
+    peers = [along_y(off) * 2 + core for off in by_distance for core in range(2)]
+    peers.append(me_p + 1 - 2 * me_c)
+
+    def sum_copy(part, peer):
         return pltpu.make_async_remote_copy(
-            src_ref=part_b.at[which, q, pl.ds(owner * per_owner, per_owner)],
-            dst_ref=recv_p.at[me_p, q],
-            send_sem=rs_send.at[owner, which, q],
-            recv_sem=rs_recv.at[me_p, q],
-            device_id=(me_s, me_r, owner * 2 + core),
+            src_ref=part_b.at[part, peer],
+            dst_ref=recv_p.at[part, me_p],
+            send_sem=rs_send.at[part, peer],
+            recv_sem=rs_recv.at[part, me_p],
+            device_id=(me_s, me_r, peer),
             device_id_type=MESH,
         )
 
-    def sum_copies(which):
-        return by_distance if which else by_distance + [0]
-
-    for which in range(2):
-        start = col0 if which else other0
-        for q in range(2):
-            cols = pl.ds(pl.multiple_of(start + q * wide, LANES), wide)
-            partial = dot(hidden, w[:, cols])
+    for part in range(PARTS):
+        for b in range(blocks_of):
+            start = b * wide + part * narrow
+            partial = dot(hidden, w[:, start : start + narrow])
             for i in range(steps):
-                rows = partial[i * held : (i + 1) * held]
-                part_b[which, q, i] = rows.astype(BF16)
-                if which:
-                    part_f[q, i] = rows
-            for off in sum_copies(which):
-                sum_copy(which, q, off).start()
+                for core in range(2):
+                    row = b * owned + (i % per_owner) * mine_each
+                    here = i * held + core * mine_each
+                    part_f[part, i // per_owner * 2 + core, row : row + mine_each, :] = partial[
+                        here : here + mine_each
+                    ]
+        part_b[part] = part_f[part].astype(BF16)
+        for peer in peers:
+            sum_copy(part, peer).start()
 
     loads["ck"].wait()
     loads["cv"].wait()
     all_bytes(recv_b, b_sem.at[1])
     scale = LOG2E / math.sqrt(LANES)
 
-    def soft(k, carry):
+    def soft(k):
         section = lax.div(dg_s[first + k], reps)
         place_of = jnp.int32(0)
         for k2 in range(held):
@@ -516,85 +532,97 @@
         mixed = dot(probs, cv[k])
         for u in range(steps):
             mixed = mixed + fresh_probs[:, u : u + 1] * fresh_values[steps + u : steps + u + 1]
-        res_s[k] = mixed.astype(BF16)
-        return carry
-
-    lax.fori_loop(0, held, soft, 0)
-    for r in range(reps):
-        send_t[r] = res_s[bound_for[r]]
-    to_groups(send_t, recv_t, t_sem)
-    loads["si"].wait()
-    loads["gain"].wait()
+        return mixed.astype(BF16)
+
+    def requests_for(r):
+        found = jnp.int32(0)
+        for k in range(held):
+            found = jnp.where(target_rep[k] == r, k, found)
+        return found
+
+    def answer_copy(peer_s, peer_r):
+        return pltpu.make_async_remote_copy(
+            src_ref=send_t.at[peer_r],
+            dst_ref=recv_t.at[me_g],
+            send_sem=t_sem.at[0],
+            recv_sem=t_sem.at[1],
+            device_id=(peer_s, peer_r, me_p),
+            device_id_type=MESH,
+        )
+
+    rep_steps = sorted(
+        ((dz, dx) for dz in (0, sections) for dx in range(across)),
+        key=lambda d: -hops(d[0], deep) - hops(d[1], across),
+    )
+    batch = max(held // 2, 1)
+    for start in range(0, held, batch):
+        chosen = rep_steps[start : start + batch]
+        targets = [rep_at[dz] + x_at[dx] for dz, dx in chosen]
+        answers = [soft(requests_for(r)) for r in targets]
+        for r, answer in zip(targets, answers):
+            send_t[r] = answer
+        for (dz, dx), r, answer in zip(chosen, targets, answers):
+            for ds in range(sections):
+                if dz or dx or ds:
+                    answer_copy(lax.rem(me_s + ds, sections), r).start()
+                else:
+                    recv_t[me_g] = answer
+
     summed = []
-    for part in range(2):
-        here = slice(part * wide, (part + 1) * wide)
-        value = part_f[part, pl.ds(y0, per_owner)] + si[:, :, here].astype(F32)
-        sources = [me_p + 1 - 2 * me_c]
-        for off in reversed(by_distance):
-            sources += [along_y(off) * 2, along_y(off) * 2 + 1]
-        for source in sources:
-            pltpu.make_async_copy(
-                recv_p.at[source, part], recv_p.at[source, part], rs_recv.at[source, part]
-            ).wait()
-            value = value + recv_p[source, part].astype(F32)
+    for part in range(PARTS):
+        here = slice(part * narrow, (part + 1) * narrow)
+        value = part_f[part, me_p] + base_of[:, here]
+        for source in reversed(peers):
+            block = recv_p.at[part, source]
+            pltpu.make_async_copy(block, block, rs_recv.at[part, source]).wait()
+            value = value + recv_p[part, source].astype(F32)
         summed.append(value)
-    square = jnp.sum(summed[0] * summed[0], axis=2, keepdims=True)
-    square = square + jnp.sum(summed[1] * summed[1], axis=2, keepdims=True)
-    ss_send[...] = jnp.broadcast_to(square, ss_send.shape)
-    squares = pltpu.make_async_remote_copy(
-        src_ref=ss_send,
-        dst_ref=ss_recv,
-        send_sem=ss_sem.at[0],
-        recv_sem=ss_sem.at[1],
-        device_id=sibling,
-        device_id_type=MESH,
-    )
-    squares.start()
-    squares.wait()
-    mean = (square + ss_recv[:, :, 0:1]) / model
-    spread_of = jnp.sqrt(mean + 1e-06)
-    def place(y, part):
-        cols = pl.ds(pl.multiple_of(col0 + part * wide, LANES), wide)
-        return do.at[pl.ds(y * per_owner, per_owner), :, cols]
-
-    def gather_copy(off, part):
-        peer = along_y(off)
+    square = jnp.sum(sum(value * value for value in summed), axis=1, keepdims=True)
+    square = jnp.broadcast_to(square, (TILE, LANES))
+    shift = TILE // 2
+    while shift >= owned:
+        square = square + pltpu.roll(square, shift, 0)
+        shift //= 2
+    spread_of = jnp.sqrt(square[:, :1] / model + 1e-06)
+
+    def gather_copy(off):
+        peer = along_y(off) * 2 + me_c
         return pltpu.make_async_remote_copy(
-            src_ref=place(me_y, part),
-            dst_ref=place(me_y, part),
-            send_sem=ag_send.at[peer, part],
-            recv_sem=ag_recv.at[me_y, part],
-            device_id=(me_s, me_r, peer * 2 + me_c),
+            src_ref=rows_of.at[me_p],
+            dst_ref=rows_of.at[me_p],
+            send_sem=ag_send.at[peer],
+            recv_sem=ag_recv.at[me_p],
+            device_id=(me_s, me_r, peer),
             device_id_type=MESH,
         )
 
-    def pass_copy(y, part):
+    def pass_copy(y):
+        source = y * 2 + me_c
         return pltpu.make_async_remote_copy(
-            src_ref=place(y, part),
-            dst_ref=place(y, part),
-            send_sem=pass_send.at[y, part],
-            recv_sem=pass_recv.at[y, part],
+            src_ref=rows_of.at[source],
+            dst_ref=rows_of.at[source],
+            send_sem=pass_send.at[y],
+            recv_sem=ag_recv.at[source],
             device_id=sibling,
             device_id_type=MESH,
         )
 
-    for part in range(2):
-        here = slice(part * wide, (part + 1) * wide)
-        gains = gain[:, here].reshape(1, 1, wide)
-        place(me_y, part)[...] = (summed[part] / spread_of * gains).astype(BF16)
-        for off in by_distance:
-            gather_copy(off, part).start()
-    for part in range(2):
-        pass_copy(me_y, part).start()
+    def landed(source):
+        block = rows_of.at[source]
+        pltpu.make_async_copy(block, block, ag_recv.at[source]).wait()
+
+    for part in range(PARTS):
+        here = slice(part * narrow, (part + 1) * narrow)
+        rows_of[me_p, part] = (summed[part] / spread_of * gain_of[:, here]).astype(BF16)
+    for off in by_distance:
+        gather_copy(off).start()
+    pass_copy(me_y).start()
 
     lax.fori_loop(early, held, prompt, 0)
 
-    for part in range(2):
-        for off in reversed(by_distance):
-            source = along_y(off)
-            landed = place(source, part)
-            pltpu.make_async_copy(landed, landed, ag_recv.at[source, part]).wait()
-            pass_copy(source, part).start()
+    for off in reversed(by_distance):
+        landed(along_y(off) * 2 + me_c)
+        pass_copy(along_y(off)).start()
 
     all_bytes(recv_t, t_sem.at[1])
     placed = dot(sel_soft[...], recv_t[...].reshape(groups * soft_rows, LANES))
@@ -608,15 +636,31 @@
     all_bytes(recv_a, a_sem.at[0])
     all_bytes(recv_b, b_sem.at[0])
     all_bytes(recv_t, t_sem.at[0])
-    for which in range(2):
-        for q in range(2):
-            for off in sum_copies(which):
-                sum_copy(which, q, off).wait_send()
-    for part in range(2):
-        for off in range(1, owners):
-            gather_copy(off, part).wait_send()
-        for y in range(owners):
-            pass_copy(y, part).wait()
+    for part in range(PARTS):
+        for peer in peers:
+            sum_copy(part, peer).wait_send()
+
+    shape = (blocks_of * per_owner * held, 2 * TILE)
+    slot = lax.rem(iota(shape, 0), held)
+    step = lax.rem(iota(shape, 0) // held, per_owner)
+    block = iota(shape, 0) // (held * per_owner)
+    wanted = (slot // mine_each) * TILE + block * owned + step * mine_each
+    unpack = one_hot(wanted + lax.rem(slot, mine_each) == iota(shape, 1))
+    for off in [0] + list(reversed(by_distance)):
+        y = along_y(off)
+        landed(y * 2 + 1 - me_c)
+        for part in range(PARTS):
+            pair = rows_of[pl.ds(y * 2, 2), part].reshape(2 * TILE, narrow)
+            ordered = dot(unpack, pair)
+            for b in range(blocks_of):
+                start = b * wide + part * narrow
+                for n in range(per_owner):
+                    rows = slice((b * per_owner + n) * held, (b * per_owner + n + 1) * held)
+                    do[y * per_owner + n, :, start : start + narrow] = ordered[rows].astype(BF16)
+    for off in by_distance:
+        gather_copy(off).wait_send()
+    for y in range(owners):
+        pass_copy(along_y(y)).wait_send()
 
 
 def write_out(po, do, so, po_hbm, do_hbm, so_hbm, sem):
@@ -657,8 +701,8 @@
     model = out_weight.shape[1]
     groups = sections * reps
     width = heads * LANES
-    half = model // 2
     per_owner = steps * 2 // tps
+    narrow = model * per_owner * (held // 2) // TILE // PARTS
     lin_rows = heads * steps
     soft_rows = q_heads * steps
     total = groups * held
@@ -697,8 +741,8 @@
         vmem((held, length, LANES), BF16),
         vmem((held, length, LANES), BF16),
         vmem((width, model), BF16),
-        vmem((1, half), F32),
-        vmem((per_owner, held, half), BF16),
+        vmem((1, model), F32),
+        vmem((per_owner, held, model), BF16),
         vmem((steps, held, width), BF16),
         vmem((steps, held, width), BF16),
         vmem((steps, held, width), BF16),
@@ -723,27 +767,25 @@
         vmem((reps, soft_rows + lin_rows, LANES), BF16),
         vmem((sections, held // sections, soft_rows + lin_rows, LANES), BF16),
         vmem((sections, held // sections, soft_rows + lin_rows, LANES), BF16),
-        vmem((held, soft_rows, LANES), BF16),
         vmem((reps, soft_rows, LANES), BF16),
         vmem((groups, soft_rows, LANES), BF16),
-        vmem((2, steps, held, half // 2), F32),
-        vmem((2, 2, steps, held, half // 2), BF16),
-        vmem((tps, 2, per_owner, held, half // 2), BF16),
-        vmem((per_owner, held, LANES), F32),
-        vmem((per_owner, held, LANES), F32),
+        vmem((PARTS, tps, TILE, narrow), F32),
+        vmem((PARTS, tps, TILE, narrow), BF16),
+        vmem((PARTS, tps, TILE, narrow), BF16),
+        vmem((TILE, PARTS * narrow), F32),
+        vmem((TILE, PARTS * narrow), F32),
+        vmem((tps, PARTS, TILE, narrow), BF16),
         dma((19,)),
         dma((2,)),
         dma((2,)),
         dma((2,)),
         dma((2,)),
         dma((2,)),
-        dma((tps // 2, 2, 2)),
-        dma((tps, 2)),
-        dma((2,)),
-        dma((tps // 2, 2)),
-        dma((tps // 2, 2)),
-        dma((tps // 2, 2)),
-        dma((tps // 2, 2)),
+        dma((PARTS, tps)),
+        dma((PARTS, tps)),
+        dma((tps,)),
+        dma((tps,)),
+        dma((tps // 2,)),
     ]
     anywhere = pl.BlockSpec(memory_space=pl.ANY)
     results = pl.pallas_call(

time: 41 us -> 39.8 us (0.971)
  Pallas kernels: 40.2 us -> 39 us
    pallas_call x1, Pallas kernels: 38.7 us -> 37.5 us  [on_device(): pl.pallas_call(functools.partial(body, dims), out_shape=(vmem((held, leng...]
where the time goes in v4:
time: 39.8 us; the launch traced here: 39.7 us
  Pallas kernels  39 us (98%)
  between operations  0.65 us (2%)
    pallas_call x1, Pallas kernels, on_device(): pl.pallas_call(functools.partial(body, dims), out_shape=(vmem((held, leng...  37.5 us
    pallas_call x1, Pallas kernels, on_device(): pl.pallas_call(write_out, out_shape=[jax.ShapeDtypeStruct(array.shape, ar...  1.54 us

profile of v4, /device:TPU:1, one launch (start us, length us, event | category | flops | bytes accessed | tf_op | source)
XLA Modules:
  0.0 39.7 jit_solution(5226602087728448177)
XLA Ops:
  0.6 37.5 %shard_map.193 = (bf16[8,256,512]{2,1,0:T(8,128)(2,1)S(1)}, bf16[4,8,6144]{2,1,0:T(8,128)(2,1)S(1)}, bf16[4,8,1024]{2,1,0:T(8,128)(2,1)S(1)}) custom-call(bf16[8,256,512]{2,1,0:T(8,128)(2,1)} %pq_hbm.1, bf16[8,256,512]{2,1,0:T(8,128)(2,1)} %pk_hbm.1, bf16[8,256,512]{2,1,0:T(8,128)(2,1)} %pv_hbm.1, f32[8,4,256]{2,1,0:T(4,128)} %bitcast.4, s32[256]{0:T(256)} %len_hbm.1, ...), custom_call_target="tpu_custom_call" | custom-call | tf_op jit(solution)/shard_map/pallas_call | solution.py:791
  38.1 1.5 %shard_map.194 = (bf16[8,256,512]{2,1,0:T(8,128)(2,1)}, bf16[4,8,6144]{2,1,0:T(8,128)(2,1)}, bf16[4,8,1024]{2,1,0:T(8,128)(2,1)}) custom-call(bf16[8,256,512]{2,1,0:T(8,128)(2,1)S(1)} %get-tuple-element.6.po, bf16[4,8,6144]{2,1,0:T(8,128)(2,1)S(1)} %get-tuple-element.7.do, bf16[4,8,1024]{2,1,0:T(8,128)(2,1)S(1)} %get-tuple-element.8.so), custom_call_target="tpu_custom_call" | custom-call | tf_op jit(solution)/shard_map/pallas_call | solution.py:806

commit v5 on v4

--- a/solution.py
+++ b/solution.py
@@ -434,7 +434,7 @@
     recv_b[me_s] = send_b[me_s]
 
     sel_soft[...] = pick(soft_rows, slot_of)
-    early = held // 2
+    early = held // 2 + held // 4
     lax.fori_loop(0, early, prompt, 0)
 
     mine_each = held // 2
@@ -554,7 +554,7 @@
         ((dz, dx) for dz in (0, sections) for dx in range(across)),
         key=lambda d: -hops(d[0], deep) - hops(d[1], across),
     )
-    batch = max(held // 2, 1)
+    batch = held
     for start in range(0, held, batch):
         chosen = rep_steps[start : start + batch]
         targets = [rep_at[dz] + x_at[dx] for dz, dx in chosen]

time: 39.8 us -> 39.4 us (0.990)
  no operation moved by 1% of the time
where the time goes in v5:
time: 39.4 us; the launch traced here: 39.3 us
  Pallas kernels  38.7 us (98%)
  between operations  0.65 us (2%)
    pallas_call x1, Pallas kernels, on_device(): pl.pallas_call(functools.partial(body, dims), out_shape=(vmem((held, leng...  37.1 us
    pallas_call x1, Pallas kernels, on_device(): pl.pallas_call(write_out, out_shape=[jax.ShapeDtypeStruct(array.shape, ar...  1.54 us

profile of v5, /device:TPU:1, one launch (start us, length us, event | category | flops | bytes accessed | tf_op | source)
XLA Modules:
  0.0 39.3 jit_solution(18047134648576131967)
XLA Ops:
  0.6 37.1 %shard_map.193 = (bf16[8,256,512]{2,1,0:T(8,128)(2,1)S(1)}, bf16[4,8,6144]{2,1,0:T(8,128)(2,1)S(1)}, bf16[4,8,1024]{2,1,0:T(8,128)(2,1)S(1)}) custom-call(bf16[8,256,512]{2,1,0:T(8,128)(2,1)} %pq_hbm.1, bf16[8,256,512]{2,1,0:T(8,128)(2,1)} %pk_hbm.1, bf16[8,256,512]{2,1,0:T(8,128)(2,1)} %pv_hbm.1, f32[8,4,256]{2,1,0:T(4,128)} %bitcast.4, s32[256]{0:T(256)} %len_hbm.1, ...), custom_call_target="tpu_custom_call" | custom-call | tf_op jit(solution)/shard_map/pallas_call | solution.py:791
  37.8 1.5 %shard_map.194 = (bf16[8,256,512]{2,1,0:T(8,128)(2,1)}, bf16[4,8,6144]{2,1,0:T(8,128)(2,1)}, bf16[4,8,1024]{2,1,0:T(8,128)(2,1)}) custom-call(bf16[8,256,512]{2,1,0:T(8,128)(2,1)S(1)} %get-tuple-element.6.po, bf16[4,8,6144]{2,1,0:T(8,128)(2,1)S(1)} %get-tuple-element.7.do, bf16[4,8,1024]{2,1,0:T(8,128)(2,1)S(1)} %get-tuple-element.8.so), custom_call_target="tpu_custom_call" | custom-call | tf_op jit(solution)/shard_map/pallas_call | solution.py:806
